TPU v7x, 32 devices: a whole 2x2x4 slice. The times are simulated.
32 devices in a mesh: dp: 8 (over z, x), seq: 4 (over y, core).
Axes of the slice: x: 2, y: 2, z: 4, core: 2. Of those that a mesh axis runs over, the one named last changes fastest.
Arguments:
- block_input: bfloat16 [2, 4096, 1024], P(None, ('dp', 'seq')), may hold values from -6 to 6
- positions: int32 [2, 4096], P(None, ('dp', 'seq')), may hold values from 0 to 249, as said below
- out_grad: bfloat16 [2, 4096, 1024], P(None, ('dp', 'seq')), may hold values from -6 to 6
- qkv_weight: bfloat16 [1024, 3072], P(('dp', 'seq')), may hold values from -0.1875 to 0.1875
- out_weight: bfloat16 [1024, 1024], P(('dp', 'seq')), may hold values from -1 to 1
- gate_weight: bfloat16 [1024, 4096], P(('dp', 'seq')), may hold values from -0.1875 to 0.1875
- up_weight: bfloat16 [1024, 4096], P(('dp', 'seq')), may hold values from -0.1875 to 0.1875
- down_weight: bfloat16 [4096, 1024], P(None, ('dp', 'seq')), may hold values from -0.125 to 0.125
- norm1_gain: bfloat16 [1024], P(('dp', 'seq')), may hold values from 0.5 to 1.5
- norm1_shift: bfloat16 [1024], P(('dp', 'seq')), may hold values from -2 to 2
- norm2_gain: bfloat16 [1024], P(('dp', 'seq')), may hold values from 0.5 to 1.5
- norm2_shift: bfloat16 [1024], P(('dp', 'seq')), may hold values from -2 to 2
- attn_scale: bfloat16 [1024], P(('dp', 'seq')), may hold values from 0.5 to 2
- mlp_scale: bfloat16 [1024], P(('dp', 'seq')), may hold values from 0.5 to 2
Outputs:
- output: bfloat16 [2, 4096, 1024], P(None, ('dp', 'seq'))
- input_grad: bfloat16 [2, 4096, 1024], P(None, ('dp', 'seq'))
- grad_qkv_weight: float32 [1024, 3072], P(('dp', 'seq'))
- grad_out_weight: float32 [1024, 1024], P(('dp', 'seq'))
- grad_gate_weight: float32 [1024, 4096], P(('dp', 'seq'))
- grad_up_weight: float32 [1024, 4096], P(('dp', 'seq'))
- grad_down_weight: float32 [4096, 1024], P(None, ('dp', 'seq'))
- grad_norm1_gain: float32 [1024], P(('dp', 'seq'))
- grad_norm1_shift: float32 [1024], P(('dp', 'seq'))
- grad_norm2_gain: float32 [1024], P(('dp', 'seq'))
- grad_norm2_shift: float32 [1024], P(('dp', 'seq'))
- grad_attn_scale: float32 [1024], P(('dp', 'seq'))
- grad_mlp_scale: float32 [1024], P(('dp', 'seq'))
Inputs may be any that keep to these rules, and one draw needn't show every extreme that they name: Within a clip positions count up by one from 0; clips have 125 or 250 frames, laid end to end along the frames of a micro-batch; the clip of a micro-batch's first frame may begin before it, and the last clip may be cut.
All inputs are finite; a program needn't handle non-finite values.
Results may differ from a plain program's by a relative error of at most 0.02.
Values may be sent and summed in bfloat16 or wider, within the bound.
A program may use at most 512 MiB of HBM per device.

v0:
```python
import jax
import jax.numpy as jnp
from jax import lax
from jax.sharding import PartitionSpec as P

H = 16
HD = 64
WINDOW = 128


EPSILON = 1e-05
NEGATIVE = -1e30


def normalize(values, gain, shift):
    center = values - jnp.mean(values, axis=-1, keepdims=True)
    inverse = lax.rsqrt(jnp.mean(center * center, axis=-1, keepdims=True) + EPSILON)
    unit = center * inverse
    return (unit * gain + shift, unit, inverse)


def normalize_back(incoming, unit, inverse, gain):
    scaled = incoming * gain
    middle = (
        scaled
        - jnp.mean(scaled, axis=-1, keepdims=True)
        - unit * jnp.mean(scaled * unit, axis=-1, keepdims=True)
    )
    return (inverse * middle, jnp.sum(incoming * unit, axis=0), jnp.sum(incoming, axis=0))


def angles_of(places, size):
    inverse = 10000.0 ** (-(jnp.arange(size // 2, dtype=jnp.float32) * (2.0 / size)))
    return places.astype(jnp.float32)[:, None] * inverse[None, :]


def rotate(values, angles):
    half = values.shape[-1] // 2
    cosine = jnp.cos(angles)[:, None, :]
    sine = jnp.sin(angles)[:, None, :]
    first_half = values[..., :half]
    second_half = values[..., half:]
    return jnp.concatenate(
        [first_half * cosine - second_half * sine, second_half * cosine + first_half * sine],
        axis=-1,
    )


def unrotate(values, angles):
    half = values.shape[-1] // 2
    cosine = jnp.cos(angles)[:, None, :]
    sine = jnp.sin(angles)[:, None, :]
    first_half = values[..., :half]
    second_half = values[..., half:]
    return jnp.concatenate(
        [first_half * cosine + second_half * sine, second_half * cosine - first_half * sine],
        axis=-1,
    )


def pack_shards(shards):
    return jnp.concatenate([item.reshape(1, -1) for item in shards], axis=1)


def unpack_gathered(whole, shards):
    devices = whole.shape[0]
    result = []
    offset = 0
    for number, item in enumerate(shards):
        count = item.size
        piece = whole[:, offset : offset + count]
        offset = offset + count
        if number == 4:
            rows, cols = item.shape
            result.append(
                piece.reshape(devices, rows, cols).transpose(1, 0, 2).reshape(rows, devices * cols)
            )
        elif item.ndim == 2:
            result.append(piece.reshape(devices * item.shape[0], item.shape[1]))
        else:
            result.append(piece.reshape(-1))
    return tuple(result)


def pack_grads(totals, devices):
    pieces = []
    for number, item in enumerate(totals):
        if number == 4:
            rows, cols = item.shape
            pieces.append(
                item.reshape(rows, devices, cols // devices).transpose(1, 0, 2).reshape(devices, -1)
            )
        else:
            pieces.append(item.reshape(devices, -1))
    return jnp.concatenate(pieces, axis=1)


def unpack_summed(summed, shards):
    flat = summed.reshape(-1)
    result = []
    offset = 0
    for item in shards:
        count = item.size
        result.append(flat[offset : offset + count].reshape(item.shape))
        offset = offset + count
    return tuple(result)


def block_scores(query, keys_padded, values_padded, starts, first, size):
    block_query = lax.dynamic_slice_in_dim(query, first, size, 0)
    block_keys = lax.dynamic_slice_in_dim(keys_padded, first, size + WINDOW, 0)
    block_values = lax.dynamic_slice_in_dim(values_padded, first, size + WINDOW, 0)
    begin = lax.dynamic_slice_in_dim(starts, first, size, 0)
    here = first + jnp.arange(size, dtype=jnp.int32)
    there = first - WINDOW + jnp.arange(size + WINDOW, dtype=jnp.int32)
    allowed = (
        (there[None, :] >= begin[:, None])
        & (there[None, :] <= here[:, None])
        & (here[:, None] - there[None, :] < WINDOW)
    )
    raw = jnp.einsum("qhd,khd->hqk", block_query, block_keys, preferred_element_type=jnp.float32)
    scores = jnp.where(allowed[None], raw * HD ** (-0.5), NEGATIVE)
    return (scores, block_query, block_keys, block_values)


def attend_forward(query, keys_padded, values_padded, starts):
    length = query.shape[0]
    size = min(512, length)
    count = length // size

    def step(carry, index):
        scores, block_query, block_keys, block_values = block_scores(
            query, keys_padded, values_padded, starts, index * size, size
        )
        top = jnp.max(scores, axis=-1, keepdims=True)
        exponent = jnp.exp(scores - top)
        total = jnp.sum(exponent, axis=-1, keepdims=True)
        probs = (exponent / total).astype(jnp.bfloat16)
        outcome = jnp.einsum(
            "hqk,khd->qhd", probs, block_values, preferred_element_type=jnp.float32
        )
        return (carry, (outcome, (top + jnp.log(total))[..., 0]))

    unused, (outcomes, logs) = lax.scan(step, 0, jnp.arange(count, dtype=jnp.int32))
    return (outcomes.reshape(query.shape), logs)


def attend_backward(query, keys_padded, values_padded, starts, logs, grad_out):
    length = query.shape[0]
    size = min(512, length)
    count = length // size

    def step(carry, index):
        grad_query, grad_keys, grad_values = carry
        first = index * size
        scores, block_query, block_keys, block_values = block_scores(
            query, keys_padded, values_padded, starts, first, size
        )
        probs = jnp.exp(scores - logs[index][..., None])
        grad_block = lax.dynamic_slice_in_dim(grad_out, first, size, 0)
        grad_probs = jnp.einsum(
            "qhd,khd->hqk", grad_block, block_values, preferred_element_type=jnp.float32
        )
        inner = jnp.sum(probs * grad_probs, axis=-1, keepdims=True)
        grad_scores = (probs * (grad_probs - inner) * HD ** (-0.5)).astype(jnp.bfloat16)
        query_part = jnp.einsum(
            "hqk,khd->qhd", grad_scores, block_keys, preferred_element_type=jnp.float32
        )
        keys_part = jnp.einsum(
            "hqk,qhd->khd", grad_scores, block_query, preferred_element_type=jnp.float32
        )
        values_part = jnp.einsum(
            "hqk,qhd->khd",
            probs.astype(jnp.bfloat16),
            grad_block,
            preferred_element_type=jnp.float32,
        )
        grad_query = lax.dynamic_update_slice_in_dim(grad_query, query_part, first, 0)
        grad_keys = lax.dynamic_update_slice_in_dim(
            grad_keys,
            lax.dynamic_slice_in_dim(grad_keys, first, size + WINDOW, 0) + keys_part,
            first,
            0,
        )
        grad_values = lax.dynamic_update_slice_in_dim(
            grad_values,
            lax.dynamic_slice_in_dim(grad_values, first, size + WINDOW, 0) + values_part,
            first,
            0,
        )
        return ((grad_query, grad_keys, grad_values), None)

    start_state = (
        jnp.zeros(query.shape, jnp.float32),
        jnp.zeros(keys_padded.shape, jnp.float32),
        jnp.zeros(values_padded.shape, jnp.float32),
    )
    (grad_query, grad_keys, grad_values), unused = lax.scan(
        step, start_state, jnp.arange(count, dtype=jnp.int32)
    )
    return (grad_query, grad_keys, grad_values)


def attention_forward(query, keyset, valueset, places):
    rows, heads, depth = query.shape
    width = heads * depth
    parts = lax.axis_size("seq")
    slab = width // parts
    local = slab // depth
    packed = jnp.stack(
        [query.reshape(rows, width), keyset.reshape(rows, width), valueset], axis=1
    ).reshape(rows, 3, parts, slab)
    moved = lax.all_to_all(packed, "seq", split_axis=2, concat_axis=0, tiled=True)
    group = moved.shape[0]
    every = lax.all_gather(places, "seq", axis=0, tiled=True)
    starts = jnp.maximum(jnp.arange(group, dtype=jnp.int32) - every, 0)
    padding = jnp.zeros((WINDOW, local, depth), jnp.bfloat16)
    head_query = moved[:, 0, 0].reshape(group, local, depth)
    keys_padded = jnp.concatenate([padding, moved[:, 1, 0].reshape(group, local, depth)], axis=0)
    values_padded = jnp.concatenate([padding, moved[:, 2, 0].reshape(group, local, depth)], axis=0)
    outcome, logs = attend_forward(head_query, keys_padded, values_padded, starts)
    sent = outcome.astype(jnp.bfloat16).reshape(group, 1, slab)
    attended = lax.all_to_all(sent, "seq", split_axis=0, concat_axis=1, tiled=True).reshape(
        rows, width
    )
    return (attended, (head_query, keys_padded, values_padded, starts, logs))


def attention_backward(kept, grad_attended, rows, width):
    head_query, keys_padded, values_padded, starts, logs = kept
    depth = head_query.shape[-1]
    parts = lax.axis_size("seq")
    slab = width // parts
    local = slab // depth
    came = lax.all_to_all(
        grad_attended.reshape(rows, parts, slab), "seq", split_axis=1, concat_axis=0, tiled=True
    )
    group = came.shape[0]
    grad_out = came.reshape(group, local, depth)
    grad_query, grad_keys, grad_values = attend_backward(
        head_query, keys_padded, values_padded, starts, logs, grad_out
    )
    packed = (
        jnp.stack([grad_query, grad_keys[WINDOW:], grad_values[WINDOW:]], axis=1)
        .astype(jnp.bfloat16)
        .reshape(group, 3, 1, slab)
    )
    back = lax.all_to_all(packed, "seq", split_axis=0, concat_axis=2, tiled=True).reshape(
        rows, 3, width
    )
    return (back[:, 0], back[:, 1], back[:, 2])


def forward_micro(weights, block, places):
    (
        qkv_weight,
        out_weight,
        gate_weight,
        up_weight,
        down_weight,
        gain1,
        shift1,
        gain2,
        shift2,
        scale1,
        scale2,
    ) = weights
    rows, width = block.shape
    start_in = block.astype(jnp.float32)
    normed1, unit1, inverse1 = normalize(start_in, gain1, shift1)
    acted1 = normed1.astype(jnp.bfloat16)
    projected = jnp.dot(acted1, qkv_weight, preferred_element_type=jnp.float32)
    angles = angles_of(places, HD)
    query = rotate(projected[:, :width].reshape(rows, H, HD), angles).astype(jnp.bfloat16)
    keyset = rotate(projected[:, width : 2 * width].reshape(rows, H, HD), angles).astype(
        jnp.bfloat16
    )
    valueset = projected[:, 2 * width :].astype(jnp.bfloat16)
    attended, kept = attention_forward(query, keyset, valueset, places)
    attn = jnp.dot(attended, out_weight, preferred_element_type=jnp.float32)
    mid = start_in + scale1 * attn
    normed2, unit2, inverse2 = normalize(mid, gain2, shift2)
    acted2 = normed2.astype(jnp.bfloat16)
    gate = jnp.dot(acted2, gate_weight, preferred_element_type=jnp.float32)
    up_value = jnp.dot(acted2, up_weight, preferred_element_type=jnp.float32)
    hidden = (jax.nn.silu(gate) * up_value).astype(jnp.bfloat16)
    branch = jnp.dot(hidden, down_weight, preferred_element_type=jnp.float32)
    result = (mid + scale2 * branch).astype(jnp.bfloat16)
    saved = (
        acted1,
        unit1,
        inverse1,
        angles,
        kept,
        attended,
        attn,
        unit2,
        inverse2,
        acted2,
        gate,
        up_value,
        hidden,
        branch,
    )
    return (result, saved)


def backward_micro(weights, saved, cotangent):
    (
        qkv_weight,
        out_weight,
        gate_weight,
        up_weight,
        down_weight,
        gain1,
        shift1,
        gain2,
        shift2,
        scale1,
        scale2,
    ) = weights
    (
        acted1,
        unit1,
        inverse1,
        angles,
        kept,
        attended,
        attn,
        unit2,
        inverse2,
        acted2,
        gate,
        up_value,
        hidden,
        branch,
    ) = saved
    rows, width = attended.shape
    flow = cotangent.astype(jnp.float32)
    grad_branch = (scale2 * flow).astype(jnp.bfloat16)
    grad_scale2 = jnp.sum(flow * branch, axis=0)
    grad_down = jnp.einsum("rf,rd->fd", hidden, grad_branch, preferred_element_type=jnp.float32)
    grad_hidden = jnp.einsum(
        "rd,fd->rf", grad_branch, down_weight, preferred_element_type=jnp.float32
    )
    sigmoid_gate = jax.nn.sigmoid(gate)
    grad_gate = (
        grad_hidden * up_value * sigmoid_gate * (1.0 + gate * (1.0 - sigmoid_gate))
    ).astype(jnp.bfloat16)
    grad_up = (grad_hidden * gate * sigmoid_gate).astype(jnp.bfloat16)
    grad_gate_w = jnp.einsum("rd,rf->df", acted2, grad_gate, preferred_element_type=jnp.float32)
    grad_up_w = jnp.einsum("rd,rf->df", acted2, grad_up, preferred_element_type=jnp.float32)
    grad_acted2 = jnp.einsum(
        "rf,df->rd", grad_gate, gate_weight, preferred_element_type=jnp.float32
    ) + jnp.einsum("rf,df->rd", grad_up, up_weight, preferred_element_type=jnp.float32)
    grad_mid, grad_gain2, grad_shift2 = normalize_back(grad_acted2, unit2, inverse2, gain2)
    grad_mid = flow + grad_mid
    grad_scale1 = jnp.sum(grad_mid * attn, axis=0)
    grad_attn = (scale1 * grad_mid).astype(jnp.bfloat16)
    grad_out_w = jnp.einsum("rd,re->de", attended, grad_attn, preferred_element_type=jnp.float32)
    grad_attended = jnp.einsum(
        "re,de->rd", grad_attn, out_weight, preferred_element_type=jnp.float32
    ).astype(jnp.bfloat16)
    grad_query, grad_keys, grad_values = attention_backward(kept, grad_attended, rows, width)
    query_plain = unrotate(grad_query.astype(jnp.float32).reshape(rows, H, HD), angles).reshape(
        rows, width
    )
    keys_plain = unrotate(grad_keys.astype(jnp.float32).reshape(rows, H, HD), angles).reshape(
        rows, width
    )
    grad_projected = jnp.concatenate(
        [query_plain, keys_plain, grad_values.astype(jnp.float32)], axis=1
    ).astype(jnp.bfloat16)
    grad_qkv_w = jnp.einsum("rd,re->de", acted1, grad_projected, preferred_element_type=jnp.float32)
    grad_acted1 = jnp.einsum(
        "re,de->rd", grad_projected, qkv_weight, preferred_element_type=jnp.float32
    )
    grad_first, grad_gain1, grad_shift1 = normalize_back(grad_acted1, unit1, inverse1, gain1)
    grad_input = (grad_mid + grad_first).astype(jnp.bfloat16)
    terms = (
        grad_qkv_w,
        grad_out_w,
        grad_gate_w,
        grad_up_w,
        grad_down,
        grad_gain1,
        grad_shift1,
        grad_gain2,
        grad_shift2,
        grad_scale1,
        grad_scale2,
    )
    return (grad_input, terms)


def body(
    block_input,
    positions,
    out_grad,
    qkv_weight,
    out_weight,
    gate_weight,
    up_weight,
    down_weight,
    norm1_gain,
    norm1_shift,
    norm2_gain,
    norm2_shift,
    attn_scale,
    mlp_scale,
):
    shards = (
        qkv_weight,
        out_weight,
        gate_weight,
        up_weight,
        down_weight,
        norm1_gain,
        norm1_shift,
        norm2_gain,
        norm2_shift,
        attn_scale,
        mlp_scale,
    )
    devices = lax.axis_size(("dp", "seq"))
    outer = lax.axis_size("dp")
    inner = lax.axis_size("seq")
    packed = pack_shards(shards)
    totals = None
    results = []
    grads_in = []
    for index in range(block_input.shape[0]):
        weights = unpack_gathered(lax.all_gather(packed, ("dp", "seq"), axis=0, tiled=True), shards)
        result, saved = forward_micro(weights, block_input[index], positions[index])
        backward_weights = unpack_gathered(
            lax.all_gather(packed, ("dp", "seq"), axis=0, tiled=True), shards
        )
        grad_input, terms = backward_micro(backward_weights, saved, out_grad[index])
        if totals is None:
            totals = terms
        else:
            totals = tuple(
                (first_term + second_term for first_term, second_term in zip(totals, terms))
            )
        results.append(result)
        grads_in.append(grad_input)
    laid = pack_grads(totals, devices)
    laid = laid.reshape(outer, inner, laid.shape[1])
    partial_sum = lax.psum_scatter(laid.astype(jnp.bfloat16), "dp", scatter_dimension=0, tiled=True)
    summed = lax.psum_scatter(partial_sum, "seq", scatter_dimension=1, tiled=True).astype(
        jnp.float32
    )
    return (jnp.stack(results), jnp.stack(grads_in)) + unpack_summed(summed, shards)


def solution(mesh):
    return jax.shard_map(
        body,
        mesh=mesh,
        in_specs=(
            P(None, ("dp", "seq"), None),
            P(None, ("dp", "seq")),
            P(None, ("dp", "seq"), None),
            P(("dp", "seq"), None),
            P(("dp", "seq"), None),
            P(("dp", "seq"), None),
            P(("dp", "seq"), None),
            P(None, ("dp", "seq")),
            P(("dp", "seq")),
            P(("dp", "seq")),
            P(("dp", "seq")),
            P(("dp", "seq")),
            P(("dp", "seq")),
            P(("dp", "seq")),
        ),
        out_specs=(
            P(None, ("dp", "seq"), None),
            P(None, ("dp", "seq"), None),
            P(("dp", "seq"), None),
            P(("dp", "seq"), None),
            P(("dp", "seq"), None),
            P(("dp", "seq"), None),
            P(None, ("dp", "seq")),
            P(("dp", "seq")),
            P(("dp", "seq")),
            P(("dp", "seq")),
            P(("dp", "seq")),
            P(("dp", "seq")),
            P(("dp", "seq")),
        ),
        check_vma=False,
    )
```

profile of v0, /device:TPU:0, one launch (start us, length us, event | category | flops | bytes accessed | tf_op | source)
XLA Modules:
  0.0 2108.9 jit_solution(5609141745785349704)
XLA Ops:
  28.9 6.0 all-gather
  34.9 5.5 all-gather.1
  42.8 345.4 %all-gather.5.cloned.1.call-done = bf16[32,1,524480]{2,1,0:T(2,128)(2,1)} async-done(((bf16[1,1,524480]{2,1,0:T(2,128)(2,1)}), bf16[32,1,524480]{2,1,0:T(2,128)(2,1)}) %all-gather.5.cloned.1.call-update) | async-done | bytes 33566736 | tf_op jit(solution)/shard_map/all_gather | solution.py:433
  388.2 33.4 %copy.244 = bf16[32,1,524480]{2,0,1:T(8,128)(2,1)} copy(bf16[32,1,524480]{2,1,0:T(2,128)(2,1)} %all-gather.5.cloned.1.call-done) | data formatting | bytes 67133440
  422.6 5.8 slice.331
  428.4 7.2 reshape.981
  446.7 16.7 fusion.223
  481.4 8.9 reshape.986
  490.3 8.9 reshape.987
  499.2 45.1 %reshape.988 = bf16[32,4096,32]{2,1,0:T(8,128)(2,1)} reshape(bf16[32,131072]{1,0:T(8,128)(2,1)} %get-tuple-element.234) | data formatting | bytes 16777216 | tf_op jit(solution)/shard_map/reshape | solution.py:76
  544.3 28.7 %copy.201 = bf16[4096,32,32]{0,2,1:T(8,128)(2,1)} copy(bf16[4096,32,32]{2,0,1:T(8,128)(2,1)} %bitcast.340) | data formatting | bytes 16777216 | tf_op jit(solution)/shard_map/transpose | solution.py:76
  573.1 4.6 all-to-all-start
  589.9 4.1 all-to-all-start.3
  606.9 4.1 all-to-all-start.1
  612.4 4.7 all-to-all-done.1
  622.8 5.0 fusion.235
  636.1 4.4 multiply_convert_fusion.2
  640.5 5.0 fusion.237
  645.5 6.7 multiply_convert_fusion.4
  652.1 4.1 fusion.238
  656.3 4.9 fusion.239
  661.2 4.2 convolution_add_fusion.1
  677.6 8.1 fusion.240
  685.7 8.1 fusion.241
  693.8 8.1 fusion.162
  703.5 4.2 all-to-all-start.6
  714.5 11.4 add_convert_fusion.2
  725.9 11.3 concatenate.105
  737.2 11.4 add_convert_fusion.1
  748.6 11.3 concatenate.106
  759.9 11.4 add_convert_fusion
  771.3 27.6 %copy.226 = bf16[4096,32,32]{2,0,1:T(8,128)(2,1)} copy(bf16[4096,32,32]{0,2,1:T(8,128)(2,1)} %bitcast.354) | data formatting | bytes 16777216 | tf_op jit(solution)/shard_map/reshape | solution.py:91
  799.0 37.8 %concatenate.107 = bf16[8,4,131072]{2,1,0:T(4,128)(2,1)} reshape(bf16[32,4096,32]{2,1,0:T(8,128)(2,1)} %bitcast.341) | data formatting | bytes 16777216 | tf_op jit(solution)/shard_map/concatenate | solution.py:95
  848.4 15.6 fusion.71
  864.0 18.0 fusion.62
  897.7 15.6 fusion.68
  913.7 18.0 fusion.65
  943.2 9.7 all-to-all-done.5
  965.4 4.7 add_convert_fusion.3
  970.2 9.7 concatenate.103
  979.8 7.7 constant_dynamic-update-slice_fusion.9
  989.8 9.4 constant_dynamic-update-slice_fusion.7
  999.3 4.5 constant_dynamic-update-slice_fusion.6
  1003.8 4.6 constant_dynamic-update-slice_fusion.5
  1021.7 971.3 %all-reduce.9.cloned.1.call-done = bf16[8,4,524480]{2,1,0:T(4,128)(2,1)} async-done(((bf16[8,4,524480]{2,1,0:T(4,128)(2,1)}), bf16[8,4,524480]{2,1,0:T(4,128)(2,1)}) %all-reduce.9.cloned.1.call-update) | async-done | bytes 33566736
  1993.1 7.5 constant_dynamic-slice_fusion
  2003.4 82.3 %all-reduce.11.cloned.1.call-done = bf16[1,4,524480]{2,1,0:T(4,128)(2,1)} async-done(((bf16[1,4,524480]{2,1,0:T(4,128)(2,1)}), bf16[1,4,524480]{2,1,0:T(4,128)(2,1)}) %all-reduce.11.cloned.1.call-update) | async-done | bytes 4195856
  2085.7 5.3 dynamic-slice_convert_fusion
  (403 shorter events, 195.0 us)
Async XLA Ops:
  7.2 13.3 copy-start.71
  7.2 14.6 copy-start.72
  7.2 16.1 copy-start.73
  7.2 17.5 copy-start.74
  7.2 19.0 copy-start.75
  7.2 20.3 copy-start.76
  7.2 381.0 %all-gather.5.cloned.1.call-start = ((), (), s32[]{:S(2)}) async-start(), calls=%async_computation.8 | async-start | bytes 69239808 | tf_op jit(solution)/shard_map/all_gather | solution.py:433
  9.7 19.2 copy-start.70
  9.7 30.7 %copy-start.2 = (bf16[2,128,1024]{2,1,0:T(8,128)(2,1)S(1)}, bf16[2,128,1024]{2,1,0:T(8,128)(2,1)}, u32[]{:S(2)}) copy-start(bf16[2,128,1024]{2,1,0:T(8,128)(2,1)} %param.14) | copy-start | bytes 1572868
  40.6 395.2 %copy-start.64 = (f32[128]{0:T(128)}, f32[128]{0:T(128)S(1)}, u32[]{:S(2)}) copy-start(f32[128]{0:T(128)S(1)} %get-tuple-element.325) | copy-start | bytes 1540
  40.6 403.3 %copy-start.62 = (f32[128]{0:T(128)}, f32[128]{0:T(128)S(1)}, u32[]{:S(2)}) copy-start(f32[128]{0:T(128)S(1)} %get-tuple-element.326) | copy-start | bytes 1540
  40.9 394.9 %copy-start.68 = (f32[128]{0:T(128)}, f32[128]{0:T(128)S(1)}, u32[]{:S(2)}) copy-start(f32[128]{0:T(128)S(1)} %add_rsqrt_fusion.1) | copy-start | bytes 1540
  40.9 402.9 %copy-start.66 = (f32[128]{0:T(128)}, f32[128]{0:T(128)S(1)}, u32[]{:S(2)}) copy-start(f32[128]{0:T(128)S(1)} %add_rsqrt_fusion.3) | copy-start | bytes 1540
  41.1 422.9 %copy-start.58 = (f32[128,32]{0,1:T(8,128)}, f32[128,32]{0,1:T(8,128)S(1)}, u32[]{:S(2)}) copy-start(f32[128,32]{0,1:T(8,128)S(1)} %get-tuple-element.317) | copy-start | bytes 49156
  41.2 422.9 %copy-start.60 = (f32[128,32]{0,1:T(8,128)}, f32[128,32]{0,1:T(8,128)S(1)}, u32[]{:S(2)}) copy-start(f32[128,32]{0,1:T(8,128)S(1)} %get-tuple-element.318) | copy-start | bytes 49156
  41.2 436.7 %copy-start.54 = (f32[128,32]{0,1:T(8,128)}, f32[128,32]{0,1:T(8,128)S(1)}, u32[]{:S(2)}) copy-start(f32[128,32]{0,1:T(8,128)S(1)} %get-tuple-element.309) | copy-start | bytes 49156
  41.2 436.7 %copy-start.56 = (f32[128,32]{0,1:T(8,128)}, f32[128,32]{0,1:T(8,128)S(1)}, u32[]{:S(2)}) copy-start(f32[128,32]{0,1:T(8,128)S(1)} %get-tuple-element.310) | copy-start | bytes 49156
  446.7 16.9 copy-start.32
  465.4 107.7 %all-to-all-start.2 = ((bf16[128,3,4,256]{0,3,1,2:T(8,128)(2,1)}), bf16[128,3,4,256]{0,3,1,2:T(8,128)(2,1)S(1)}, u32[]{:S(2)}, u32[]{:S(2)}) async-start(bf16[128,3,4,256]{0,3,1,2:T(8,128)(2,1)} %copy.205), calls=%async_computation.2 | async-start | bytes 1572864 | tf_op jit(solution)/shard_map/all_to_all | solution.py:213
  573.1 16.8 all-to-all-start
  589.9 17.0 all-to-all-start.3
  606.9 10.2 all-to-all-start.1
  622.8 10.6 copy-start.6
  674.0 27.9 %copy-start.9 = (f32[128,1024]{1,0:T(8,128)}, f32[128,1024]{1,0:T(8,128)S(1)}, u32[]{:S(2)}) copy-start(f32[128,1024]{1,0:T(8,128)S(1)} %get-tuple-element.284) | copy-start | bytes 1572868
  703.5 133.4 %all-to-all-start.6 = ((bf16[128,4,256]{2,0,1:T(8,128)(2,1)}), bf16[128,4,256]{2,0,1:T(8,128)(2,1)}, u32[]{:S(2)}, u32[]{:S(2)}) async-start(bf16[128,4,256]{2,0,1:T(8,128)(2,1)} %bitcast.330), calls=%async_computation.6 | async-start | bytes 524288 | tf_op jit(solution)/shard_map/all_to_all | solution.py:235
  725.9 11.3 copy-start.18
  748.6 11.3 copy-start.16
  748.6 11.3 copy-start.26
  799.0 42.7 %copy-start.42 = (bf16[512,1,1,256]{0,3,2,1:T(8,128)(2,1)S(1)}, bf16[512,1,1,256]{0,3,2,1:T(8,128)(2,1)}, u32[]{:S(2)}) copy-start(bf16[512,1,1,256]{0,3,2,1:T(8,128)(2,1)} %copy-done.41) | copy-start | bytes 786436
  836.9 49.2 %all-to-all-start.4 = ((bf16[128,4,256]{2,0,1:T(8,128)(2,1)}), bf16[128,4,256]{2,0,1:T(8,128)(2,1)S(1)}, u32[]{:S(2)}, u32[]{:S(2)}) async-start(bf16[128,4,256]{2,0,1:T(8,128)(2,1)} %bitcast.331), calls=%async_computation.4 | async-start | bytes 524288 | tf_op jit(solution)/shard_map/all_to_all | solution.py:235
  848.4 15.6 copy-start.40
  886.1 48.8 %all-to-all-start.7 = ((bf16[512,3,1,256]{3,1,2,0:T(4,128)(2,1)}), bf16[512,3,1,256]{3,1,2,0:T(4,128)(2,1)S(1)}, u32[]{:S(2)}, u32[]{:S(2)}) async-start(bf16[512,3,1,256]{3,1,2,0:T(4,128)(2,1)} %pad_maximum_fusion.1), calls=%async_computation.7 | async-start | bytes 2097152 | tf_op jit(solution)/shard_map/all_to_all | solution.py:248
  897.2 16.5 copy-start.34
  935.0 18.0 all-to-all-start.5
  938.5 1054.5 %all-reduce.9.cloned.1.call-start = ((), (), s32[]{:S(2)}) async-start(), calls=%async_computation.9 | async-start | bytes 67141632
  940.2 15.4 copy-start.59
  940.2 15.5 copy-start.61
  940.2 17.3 slice-start.6
  941.5 15.7 copy-start.55
  941.5 15.7 copy-start.57
  987.7 11.5 slice-start.12
  989.8 9.4 slice-start.13
  989.8 14.0 slice-start.10
  1020.5 1065.2 %all-reduce.11.cloned.1.call-start = ((), (), s32[]{:S(2)}) async-start(), calls=%async_computation.10 | async-start | bytes 8392704
  1993.0 9.0 copy-start.10
  1993.0 9.0 copy-start.12
  1993.1 9.1 copy-start.52
  1993.1 9.0 copy-start.53
  (56 other events, 251.7 us)
Sparse Core Ops, SparseCore 0:
  29.0 359.1 all-gather.4
  1020.6 972.3 all-reduce.8
  2000.7 84.8 all-reduce.10
where the time goes:
time: 2120 us; the launch traced here: 2110 us
  waiting for transfers between devices  1410 us (67%)
  local copies, waits for them, and re-layouts  386 us (18%)
  matrix products  221 us (10%)
  starting transfers between devices  31.8 us (2%)
  other arithmetic  28.9 us (1%)
    unnamed x5, waiting for transfers between devices  1050 us
    all_gather x1, waiting for transfers between devices, body(): lax.all_gather(packed, ('dp', 'seq'), axis=0, tiled=True)  345 us
    unnamed x224, local copies, waits for them, and re-layouts  110 us
    concatenate x6, local copies, waits for them, and re-layouts, pack_grads(): return jnp.concatenate(pieces, axis=1)  74.8 us
    reshape x1, local copies, waits for them, and re-layouts, unpack_gathered(): piece.reshape(devices, rows, cols).transpose(1, 0, 2)  45.1 us
  transfers between devices with their start and end apart: 11, of which 5 were waited for; matrix products, arithmetic and copies ran while one was open for 17% of the time, Pallas kernels for 0%

commit v1 on v0

--- a/solution.py
+++ b/solution.py
@@ -1,6 +1,10 @@
 import jax
 import jax.numpy as jnp
+import ml_dtypes
+import numpy as np
 from jax import lax
+from jax.experimental import pallas as pl
+from jax.experimental.pallas import tpu as pltpu
 from jax.sharding import PartitionSpec as P
 
 H = 16
@@ -453,9 +457,982 @@
     return (jnp.stack(results), jnp.stack(grads_in)) + unpack_summed(summed, shards)
 
 
+VMEM_BYTES = 64 * 1024 * 1024
+BF = jnp.bfloat16
+F32 = jnp.float32
+MESH = pl.DeviceIdType.MESH
+TEAM = 8
+PLACES = 256
+RELATIONS = [(1, 0, 0), (0, 1, 0), (1, 1, 0), (0, 0, 1), (1, 0, 1), (0, 1, 1), (1, 1, 1)]
+ROW_TEAM = (1, 3, 5)
+LEG = (None, 0)
+
+
+def trig_table():
+    inverse = 10000.0 ** (-(np.arange(HD // 2, dtype=np.float64) * (2.0 / HD)))
+    angles = np.arange(PLACES, dtype=np.float64)[:, None] * inverse[None, :]
+    values = np.concatenate([np.cos(angles), np.sin(angles)] * 2, axis=1).astype(np.float32)
+    high = values.astype(ml_dtypes.bfloat16)
+    rest = (values - high.astype(np.float32)).astype(ml_dtypes.bfloat16)
+    return np.concatenate([high, rest], axis=1)
+
+
+def dot(a, b):
+    return lax.dot_general(a, b, (((1,), (0,)), ((), ())), preferred_element_type=F32)
+
+
+def dot_rows(a, b):
+    return lax.dot_general(a, b, (((1,), (1,)), ((), ())), preferred_element_type=F32)
+
+
+def dot_cols(a, b):
+    return lax.dot_general(a, b, (((0,), (0,)), ((), ())), preferred_element_type=F32)
+
+
+def sigmoid(v):
+    return 0.5 * jnp.tanh(0.5 * v) + 0.5
+
+
+def unit_of(values):
+    center = values - jnp.mean(values, axis=-1, keepdims=True)
+    inverse = lax.rsqrt(jnp.mean(center * center, axis=-1, keepdims=True) + EPSILON)
+    return center * inverse, inverse
+
+
+def layer_kernel(
+    x_ref, g_ref, vec_ref, table_ref, qkv_ref, out_ref, gate_ref, up_ref, down_ref,
+    y_ref, dx_ref, vg_ref, fin_a, fin_m, zq_ref, zo_ref, zg_ref, zd_ref,
+    vec_all, vecs, gacc, gv_in, gv_z, gv_send, gv_all,
+    pack_a, pack_m, w0, w1, w2, outw,
+    n1, n2, db, da, qkv, att, probs, dqs, dkv, hid, dgu,
+    send_a, recv_c, recv_d, send_b, send_a0, recv_c0, recv_d0,
+    stage_q, stage_o, stage_g, stage_d, own_q, own_o, own_g, own_d, gout, gsend,
+    side_q, side_o, keep_q, send_q, relay_g, relay_d, relay_q, relay_o,
+    mid, attn, trig, pos,
+    vec_ss, vec_rs, wr_ss, wr_rs, wa_ss, wa_rs, w_ss, w_rs, o_ss, o_rs, ga_ss, ga_rs, ag_ss, ag_rs,
+    ra_ss, ra_rs, rs_ss, rs_rs, go_ss, go_rs, sx_ss, sx_rs, z_ss, z_rs, f_ss, f_rs,
+    gv_ss, gv_rs, loc_sem,
+):
+    dp = lax.axis_index("dp")
+    sq = lax.axis_index("seq")
+    z, xi, y, c = dp // 2, dp % 2, sq // 2, sq % 2
+    me = xi * 4 + sq
+    chip = xi * 2 + y
+
+    def copy(src, dst, ss, rs, device):
+        return pltpu.make_async_remote_copy(
+            src_ref=src, dst_ref=dst, send_sem=ss, recv_sem=rs,
+            device_id=device, device_id_type=MESH,
+        )
+
+    def span(start, size):
+        return pl.ds(pl.multiple_of(start, size), size)
+
+    def team(k):
+        kx, ky, kc = RELATIONS[k]
+        xx, yy, cc = (xi + kx) % 2, (y + ky) % 2, (c + kc) % 2
+        return (z * 2 + xx, yy * 2 + cc), xx * 4 + yy * 2 + cc
+
+    def level(j):
+        zz = (z + j) % 4
+        return (zz * 2 + xi, sq), zz
+
+    teams = [team(k) for k in range(7)]
+    levels = [level(j) for j in range(1, 4)]
+    sources = [(z + 4 - j) % 4 for j in range(1, 4)]
+    across, beside, sibling = teams[0][0], teams[1][0], teams[3][0]
+    chips = [(1 - xi) * 2 + y, xi * 2 + (1 - y), (1 - xi) * 2 + (1 - y)]
+
+    pending = []
+    pack_sends = []
+    barrier = pltpu.get_barrier_semaphore()
+    for device, _ in teams + levels:
+        pl.semaphore_signal(barrier, inc=1, device_id=device, device_id_type=MESH)
+
+    for t in range(4):
+        for b in range(3):
+            pack_a[32 * t : 32 * t + 32, 256 * b : 256 * b + 256] = qkv_ref[
+                :, 1024 * b + 256 * t : 1024 * b + 256 * t + 256
+            ]
+        pack_a[32 * t : 32 * t + 32, 768:1024] = out_ref[:, 256 * t : 256 * t + 256]
+    lane = lax.broadcasted_iota(jnp.int32, (8, 128), 1)
+    sub = lax.broadcasted_iota(jnp.int32, (8, 128), 0)
+    vec_all[z, me] = jnp.where((sub >= 6) | (lane // 32 == me % 4), vec_ref[...], 0.0)
+    gacc[...] = jnp.zeros_like(gacc)
+    pl.semaphore_wait(barrier, 10)
+
+    def begin(item):
+        item.start()
+        pending.append(item)
+
+    for k, (device, _) in enumerate(teams):
+        begin(copy(vec_all.at[z, me], vec_all.at[z, me], vec_ss.at[k], vec_rs.at[k], device))
+
+    my_rows = span((z * 8 + me) * 32, 32)
+    w0[my_rows, :] = pack_a[span(sq * 32, 32), :]
+    for i, k in enumerate(ROW_TEAM):
+        device, g = teams[k]
+        begin(
+            copy(pack_a.at[span((g % 4) * 32, 32), :], w0.at[my_rows, :], wr_ss.at[i], wr_rs.at[i],
+                 device)
+        )
+    for t in range(TEAM):
+        pack_m[32 * t : 32 * t + 32, 0:512] = gate_ref[:, 512 * t : 512 * t + 512]
+        pack_m[32 * t : 32 * t + 32, 512:1024] = up_ref[:, 512 * t : 512 * t + 512]
+        pack_m[32 * t : 32 * t + 32, 1024:1536] = down_ref[:, 512 * t : 512 * t + 512]
+
+    jumps = [z == 3, None, z == 0]
+    passes = (z == 1) | (z == 2)
+
+    def rise(ref, piece, ss, rs, base):
+        for j in (1, 0, 2):
+            item = copy(
+                ref.at[piece(z)], ref.at[piece(z)], ss.at[base + j], rs.at[base + j], levels[j][0]
+            )
+            if jumps[j] is None:
+                begin(item)
+            else:
+                pl.when(jnp.logical_not(jumps[j]))(item.start)
+                pending.append((jumps[j], item))
+
+    def rise_pass(ref, piece, ss, rs, base):
+        arrived = ref.at[piece(sources[1])]
+        copy(arrived, arrived, ss.at[base + 1], rs.at[base + 1], levels[1][0]).wait_recv()
+        slot = jnp.where(z == 1, 0, 2)
+        end = jnp.where(z == 1, 0, 3)
+        item = copy(arrived, arrived, ss.at[base + 3], rs.at[base + slot], (end * 2 + xi, sq))
+        pl.when(passes)(item.start)
+        pending.append((jnp.logical_not(passes), item))
+
+    def rise_wait(ref, piece, ss, rs, base, j):
+        arrived = ref.at[piece(sources[j])]
+        copy(arrived, arrived, ss.at[base + j], rs.at[base + j], levels[j][0]).wait_recv()
+
+    groups = [(w1, 0, 1024), (w2, 1024, 512)]
+
+    def level_rows(zz):
+        return span(zz * 256, 256)
+
+    def weights_out(n):
+        ref, first, width = groups[n]
+        ref[my_rows, :] = pack_m[span(me * 32, 32), first : first + width]
+        for k, (device, g) in enumerate(teams):
+            item = copy(
+                pack_m.at[span(g * 32, 32), pl.ds(first, width)],
+                ref.at[my_rows, :], w_ss.at[n, k], w_rs.at[n, k], device,
+            )
+            item.start()
+            pack_sends.append(item)
+
+    def weights_up(n):
+        ref = groups[n][0]
+        for k, (device, g) in enumerate(teams):
+            rows = span((z * 8 + g) * 32, 32)
+            copy(ref.at[rows, :], ref.at[rows, :], w_ss.at[n, k], w_rs.at[n, k], device).wait_recv()
+        rise(ref, level_rows, w_ss.at[n], w_rs.at[n], 7)
+
+    def weights_pass(n):
+        rise_pass(groups[n][0], level_rows, w_ss.at[n], w_rs.at[n], 7)
+
+    def weights_in(n):
+        for j in (0, 2):
+            rise_wait(groups[n][0], level_rows, w_ss.at[n], w_rs.at[n], 7, j)
+
+    halves = [pl.ds(0, 768), pl.ds(768, 256)]
+
+    def slab(n, zz, xx):
+        return span((zz * 2 + xx) * 128, 128), halves[n]
+
+    def slab_up(n):
+        rise(w0, lambda zz: slab(n, zz, xi), wa_ss.at[n], wa_rs.at[n], 0)
+        mine = w0.at[slab(n, z, xi)]
+        begin(copy(mine, mine, wa_ss.at[n, 4], wa_rs.at[n, 4], across))
+
+    def slab_pass(n):
+        rise_pass(w0, lambda zz: slab(n, zz, xi), wa_ss.at[n], wa_rs.at[n], 0)
+        for j in (1, 0, 2):
+            if j != 1:
+                rise_wait(w0, lambda zz: slab(n, zz, xi), wa_ss.at[n], wa_rs.at[n], 0, j)
+            block = w0.at[slab(n, sources[j], xi)]
+            begin(copy(block, block, wa_ss.at[n, 5 + j], wa_rs.at[n, 5 + j], across))
+
+    def slab_in(n):
+        for j in range(4):
+            block = w0.at[slab(n, z if j == 0 else sources[j - 1], 1 - xi)]
+            copy(block, block, wa_ss.at[n, 4 + j], wa_rs.at[n, 4 + j], across).wait_recv()
+
+    for k, (device, g) in enumerate(teams):
+        copy(vec_all.at[z, g], vec_all.at[z, g], vec_ss.at[k], vec_rs.at[k], device).wait_recv()
+    for j, (device, _) in enumerate(levels):
+        begin(copy(vec_all.at[z], vec_all.at[z], vec_ss.at[7 + j], vec_rs.at[7 + j], device))
+    for i, k in enumerate(ROW_TEAM):
+        device, g = teams[k]
+        rows = w0.at[span((z * 8 + g) * 32, 32), :]
+        copy(rows, rows, wr_ss.at[i], wr_rs.at[i], device).wait_recv()
+    slab_up(0)
+    for j in range(3):
+        block = vec_all.at[sources[j]]
+        copy(block, block, vec_ss.at[7 + j], vec_rs.at[7 + j], levels[j][0]).wait_recv()
+    for k in range(8):
+        total = vec_all[k // 2, 4 * (k % 2)]
+        for j in range(1, 4):
+            total = total + vec_all[k // 2, 4 * (k % 2) + j]
+        vecs[:, 128 * k : 128 * k + 128] = total
+
+    def vector(n):
+        return vecs[n : n + 1, :]
+
+    def row_rows(m, cc, yy):
+        return span(m * 512 + cc * 256 + yy * 128, 128)
+
+    def row_start(ref, e, m):
+        block = ref.at[row_rows(m, c, y), :]
+        begin(copy(block, block, ga_ss.at[e, m, 0], ga_rs.at[e, m, 0], beside))
+        begin(copy(block, block, ga_ss.at[e, m, 1], ga_rs.at[e, m, 1], sibling))
+
+    def row_pass(ref, e, m):
+        block = ref.at[row_rows(m, c, 1 - y), :]
+        copy(block, block, ga_ss.at[e, m, 0], ga_rs.at[e, m, 0], beside).wait_recv()
+        begin(copy(block, block, ga_ss.at[e, m, 2], ga_rs.at[e, m, 2], sibling))
+
+    def row_end(ref, e, m):
+        for which, yy in ((1, y), (2, 1 - y)):
+            block = ref.at[row_rows(m, 1 - c, yy), :]
+            copy(block, block, ga_ss.at[e, m, which], ga_rs.at[e, m, which], sibling).wait_recv()
+
+    def slot_rows(m, cc, place):
+        return span(m * 1024 + cc * 512 + place * 128, 128)
+
+    def gather_start(ref, e, m):
+        block = ref.at[slot_rows(m, c, chip), :]
+        for r in (0, 1, 3):
+            begin(copy(block, block, ag_ss.at[e, m, r], ag_rs.at[e, m, r], teams[r][0]))
+
+    def gather_hand(ref, e, m, r):
+        block = ref.at[slot_rows(m, c, chips[r]), :]
+        copy(block, block, ag_ss.at[e, m, r], ag_rs.at[e, m, r], teams[r][0]).wait_recv()
+        begin(copy(block, block, ag_ss.at[e, m, 4 + r], ag_rs.at[e, m, 4 + r], sibling))
+
+    def gather_pass(ref, e, m, last):
+        first = 1 - last
+        gather_hand(ref, e, m, first)
+        block = ref.at[slot_rows(m, c, chips[first]), :]
+        begin(copy(block, block, ag_ss.at[e, m, 2], ag_rs.at[e, m, 2], teams[last][0]))
+        gather_hand(ref, e, m, last)
+
+    def gather_far(ref, e, m):
+        gather_hand(ref, e, m, 2)
+
+    def gather_end(ref, e, m):
+        for r in range(4):
+            place = chip if r == 3 else chips[r]
+            which = 3 if r == 3 else 4 + r
+            block = ref.at[slot_rows(m, 1 - c, place), :]
+            copy(block, block, ag_ss.at[e, m, which], ag_rs.at[e, m, which], sibling).wait_recv()
+
+    for m in range(2):
+        unit, _ = unit_of(x_ref[m].astype(F32))
+        n1[row_rows(m, c, y), :] = (unit * vector(0) + vector(1)).astype(BF)
+        row_start(n1, 0, m)
+    for m in range(2):
+        db[slot_rows(m, c, chip), :] = (g_ref[m].astype(F32) * vector(5)).astype(BF)
+    gather_start(db, 0, 0)
+
+    def make_trig(index, carry):
+        m, slot = index // 4, index % 4
+        cc, yy = slot // 2, slot % 2
+        row = vec_all[z, xi * 4 + yy * 2 + cc, pl.ds(6 + m, 1), :]
+        places = jnp.transpose(jnp.broadcast_to(row, (128, 128)))
+        rows = span(index * 128, 128)
+        pos[rows, :] = places
+        hits = lax.broadcasted_iota(jnp.int32, (128, PLACES), 1).astype(F32) == jnp.concatenate(
+            [places, places], axis=1
+        )
+        both = dot(hits.astype(F32).astype(BF), table_ref[...])
+        trig[rows, :] = both[:, :128] + both[:, 128:]
+        return carry
+
+    lax.fori_loop(0, 8, make_trig, 0)
+    weights_out(0)
+
+    def expand(rows, count):
+        both = trig[rows, :]
+        front = lax.broadcasted_iota(jnp.int32, (count, 128), 1) % 64 < 32
+        cosine = jnp.where(front, both, pltpu.roll(both, 32, 1))
+        sine = jnp.where(front, -pltpu.roll(both, 96, 1), both)
+        return front, cosine, sine
+
+    def swap(values, front):
+        return jnp.where(front, pltpu.roll(values, 96, 1), pltpu.roll(values, 32, 1))
+
+    slab_pass(0)
+    slab_up(1)
+    row_pass(n1, 0, 0)
+    row_pass(n1, 0, 1)
+    gather_pass(db, 0, 0, 1)
+    weights_out(1)
+    weights_up(0)
+    slab_in(0)
+
+    first_head = lax.broadcasted_iota(jnp.int32, (128, 128), 1) < 64
+
+    def split_heads(values):
+        zero = jnp.zeros_like(values)
+        return jnp.concatenate(
+            [jnp.where(first_head, values, zero), jnp.where(first_head, zero, values)], axis=0
+        )
+
+    def join_heads(values):
+        return jnp.where(first_head, values[:128], values[128:])
+
+    def project(m):
+        def step(i, carry):
+            rows = span(m * 512 + i * 256, 256)
+            raw = dot(n1[rows, :], w0[:, 0:768])
+            front, cosine, sine = expand(rows, 256)
+            for b in range(4):
+                part = raw[:, 128 * b : 128 * b + 128]
+                qkv[rows, 128 * b : 128 * b + 128] = (
+                    part * cosine + swap(part, front) * sine
+                ).astype(BF)
+            qkv[rows, 512:768] = raw[:, 512:768].astype(BF)
+            return carry
+
+        lax.fori_loop(0, 2, step, 0)
+
+    def block_rows(m, s):
+        return span(m * 512 + (s % 2) * 256 + (s // 2) * 128, 128)
+
+    def pair(b, p):
+        return slice(256 * b + 128 * p, 256 * b + 128 * p + 128)
+
+    def attend(m):
+        def step(s, carry):
+            rows = block_rows(m, s)
+            before = block_rows(m, jnp.maximum(s - 1, 0))
+            r = lax.broadcasted_iota(jnp.int32, (128, 256), 0)
+            k = lax.broadcasted_iota(jnp.int32, (128, 256), 1)
+            back = r + 128 - k
+            places = pos[rows, :]
+            limit = jnp.minimum(jnp.concatenate([places, places], axis=1).astype(jnp.int32), 127)
+            limit = jnp.minimum(limit, s * 128 + r)
+            allowed = (back >= 0) & (back <= limit)
+            allowed = jnp.concatenate([allowed, allowed], axis=0)
+            for p in range(2):
+                query = split_heads(qkv[rows, pair(0, p)])
+                keys = jnp.concatenate([qkv[before, pair(1, p)], qkv[rows, pair(1, p)]], axis=0)
+                held = jnp.concatenate([qkv[before, pair(2, p)], qkv[rows, pair(2, p)]], axis=0)
+                scores = dot_rows(query, keys) * (HD ** -0.5)
+                scores = jnp.where(allowed, scores, NEGATIVE)
+                top = jnp.max(scores, axis=-1, keepdims=True)
+                exponent = jnp.exp(scores - top)
+                total = jnp.sum(exponent, axis=-1, keepdims=True)
+                share = (exponent / total).astype(BF)
+                probs[(m * 4 + s) * 2 + p] = share
+                att[rows, pair(0, p)] = join_heads(dot(share, held)).astype(BF)
+            return carry
+
+        lax.fori_loop(0, 4, step, 0)
+
+    def row_send(e, m):
+        return copy(
+            send_a0.at[m, span((1 - y) * 128, 128), :], recv_d0.at[m], ra_ss.at[e, m, 1],
+            ra_rs.at[e, m, 1], beside,
+        )
+
+    def row_scatter(e, m, compute):
+        hand = copy(send_b.at[m], recv_c0.at[m], ra_ss.at[e, m, 0], ra_rs.at[e, m, 0], sibling)
+
+        def step(j, carry):
+            part = compute(pl.multiple_of(m * 512 + ((c + 1 + j) % 2) * 256, 256))
+
+            @pl.when(j == 0)
+            def _():
+                send_b[m] = part.astype(BF)
+                hand.start()
+
+            @pl.when(j == 1)
+            def _():
+                hand.wait_recv()
+                send_a0[m] = (part + recv_c0[m].astype(F32)).astype(BF)
+                row_send(e, m).start()
+
+            return carry
+
+        lax.fori_loop(0, 2, step, 0)
+        hand.wait_send()
+
+    def row_scatter_end(e, m):
+        row_send(e, m).wait()
+        return send_a0[m, span(y * 128, 128), :].astype(F32) + recv_d0[m].astype(F32)
+
+    def scatter(e, m, compute):
+        def step(j, carry):
+            cc = (c + 1 + j // 2) % 2
+            xx = (xi + 1 + j % 2) % 2
+            part = compute(pl.multiple_of(m * 1024 + cc * 512 + xx * 256, 256))
+            there = span(xx * 256, 256)
+
+            @pl.when(j < 2)
+            def _():
+                send_b[j] = part.astype(BF)
+                copy(
+                    send_b.at[j], recv_c.at[e, m, there, :], rs_ss.at[e, m, j], rs_rs.at[e, m, j],
+                    sibling,
+                ).start()
+
+            @pl.when(j >= 2)
+            def _():
+                copy(
+                    send_b.at[j - 2], recv_c.at[e, m, there, :], rs_ss.at[e, m, j - 2],
+                    rs_rs.at[e, m, j - 2], sibling,
+                ).wait_recv()
+                send_a[m, there, :] = (
+                    part + recv_c[e, m, there, :].astype(F32)
+                ).astype(BF)
+
+            @pl.when(j == 2)
+            def _():
+                scatter_send(e, m, 2).start()
+                if LEG[e] != 1:
+                    scatter_send(e, m, 0).start()
+
+            @pl.when(j == 3)
+            def _():
+                if LEG[e] != 0:
+                    scatter_send(e, m, 1).start()
+
+            return carry
+
+        lax.fori_loop(0, 4, step, 0)
+        for j in range(2):
+            copy(
+                send_b.at[j], recv_c.at[e, m, pl.ds(0, 256), :], rs_ss.at[e, m, j],
+                rs_rs.at[e, m, j], sibling,
+            ).wait_send()
+
+    def scatter_send(e, m, r):
+        rows = span(chips[r] * 128, 128)
+        return copy(
+            send_a.at[m, rows, :], recv_d.at[e, m, r], rs_ss.at[e, m, 2 + r],
+            rs_rs.at[e, m, 2 + r], teams[r if r < 2 or LEG[e] is None else LEG[e]][0],
+        )
+
+    def scatter_pass(e, m):
+        r = 1 - LEG[e]
+        rows = span(chips[r] * 128, 128)
+        scatter_send(e, m, 2).wait_recv()
+        send_a[m, rows, :] = (
+            send_a[m, rows, :].astype(F32) + recv_d[e, m, 2].astype(F32)
+        ).astype(BF)
+        scatter_send(e, m, r).start()
+
+    def scatter_end(e, m):
+        direct = LEG[e] is None
+        for r in range(3):
+            if r < 2 or direct:
+                scatter_send(e, m, r).wait()
+            else:
+                scatter_send(e, m, r).wait_send()
+        total = send_a[m, span(chip * 128, 128), :].astype(F32)
+        for r in range(3 if direct else 2):
+            total = total + recv_d[e, m, r].astype(F32)
+        return total
+
+    def outwards(row):
+        return dot(att[pl.ds(row, 256), :], outw[...])
+
+    row_end(n1, 0, 0)
+    project(0)
+    slab_pass(1)
+    attend(0)
+    slab_in(1)
+    for i, k in enumerate(ROW_TEAM):
+        device, g = teams[k]
+        begin(
+            copy(
+                w0.at[span((g % 4) * 256, 256), pl.ds(768, 256)],
+                outw.at[:, span(sq * 256, 256)], o_ss.at[i], o_rs.at[i], device,
+            )
+        )
+    outw[:, span(sq * 256, 256)] = w0[span(sq * 256, 256), 768:1024]
+    gather_start(db, 0, 1)
+    row_end(n1, 0, 1)
+    project(1)
+    for i, k in enumerate(ROW_TEAM):
+        device, g = teams[k]
+        copy(
+            w0.at[span((g % 4) * 256, 256), pl.ds(768, 256)],
+            outw.at[:, span((g % 4) * 256, 256)], o_ss.at[i], o_rs.at[i], device,
+        ).wait_recv()
+    row_scatter(0, 0, outwards)
+    weights_up(1)
+    attend(1)
+    row_scatter(0, 1, outwards)
+
+    def second_norm(m):
+        total = row_scatter_end(0, m)
+        attn[m] = total
+        middle = x_ref[m].astype(F32) + vector(4) * total
+        mid[m] = middle
+        unit, _ = unit_of(middle)
+        n2[slot_rows(m, c, chip), :] = (unit * vector(2) + vector(3)).astype(BF)
+
+    gather_far(db, 0, 0)
+    second_norm(0)
+    gather_start(n2, 1, 0)
+    gather_pass(db, 0, 1, 0)
+    weights_pass(0)
+    second_norm(1)
+    gather_start(n2, 1, 1)
+    gather_pass(n2, 1, 0, 0)
+    gather_far(db, 0, 1)
+    gather_far(n2, 1, 0)
+    gather_pass(n2, 1, 1, 1)
+    weights_pass(1)
+
+    def mlp(row):
+        rows = pl.ds(row, 256)
+        both = dot(n2[rows, :], w1[...])
+        d_hidden = dot(db[rows, :], w2[...])
+        gate, up = both[:, :512], both[:, 512:]
+        sig = sigmoid(gate)
+        silu = gate * sig
+        hid[rows, :] = (silu * up).astype(BF)
+        dgu[rows, 0:512] = (d_hidden * up * sig * (1.0 + gate * (1.0 - sig))).astype(BF)
+        dgu[rows, 512:1024] = (d_hidden * silu).astype(BF)
+        return dot_rows(dgu[rows, :], w1[...])
+
+    weights_in(0)
+    weights_in(1)
+    gather_end(db, 0, 0)
+    gather_end(n2, 1, 0)
+    scatter(0, 0, mlp)
+    gather_far(n2, 1, 1)
+    gather_end(db, 0, 1)
+    gather_end(n2, 1, 1)
+    scatter(0, 1, mlp)
+
+    turned = (z == 0) | (z == 2)
+    at_end = (z == 0) | (z == 3)
+
+    def target(i):
+        inner = jnp.where(i == 3, 1, jnp.where(i == 0, 0, i + 1))
+        plain = jnp.where(at_end, i, inner)
+        return jnp.where(turned, 3 - plain, plain)
+
+    def descend(n, i, stage, arrive, relay):
+        zz = target(i)
+
+        @pl.when(at_end & (i == 0))
+        def _():
+            via = jnp.where(z == 0, 1, 2)
+            copy(stage.at[i], relay, z_ss.at[n, i], z_rs.at[n, 3], (via * 2 + xi, sq)).start()
+
+        @pl.when(jnp.logical_not(at_end & (i == 0)) & (at_end | (i < 2)))
+        def _():
+            slot = (zz + 3 - z) % 4
+            copy(
+                stage.at[i], arrive.at[slot], z_ss.at[n, i], z_rs.at[n, slot], (zz * 2 + xi, sq)
+            ).start()
+
+    def descend_pass(n, stage, arrive, relay):
+        @pl.when(passes)
+        def _():
+            zz = target(2)
+            slot = (zz + 3 - z) % 4
+            copy(stage.at[2], relay, z_ss.at[n, 2], z_rs.at[n, 3], levels[0][0]).wait_recv()
+            stage[2] = (stage[2].astype(F32) + relay[...].astype(F32)).astype(BF)
+            copy(
+                stage.at[2], arrive.at[slot], z_ss.at[n, 2], z_rs.at[n, slot], (zz * 2 + xi, sq)
+            ).start()
+
+    def weight_grad(n, left, right, stage, own, arrive, relay):
+        def step(i, carry):
+            part = dot_cols(left[:, span(target(i) * 256, 256)], right[...])
+
+            @pl.when(i < 3)
+            def _():
+                stage[i] = part.astype(BF)
+                descend(n, i, stage, arrive, relay)
+
+            @pl.when(i == 3)
+            def _():
+                own[...] = part.astype(own.dtype)
+
+            return carry
+
+        lax.fori_loop(0, 4, step, 0)
+
+    weight_grad(0, n2, dgu, stage_g, own_g, zg_ref, relay_g)
+
+    def norm_back(grad, values, gain, row):
+        unit, inverse = unit_of(values)
+        gacc[row : row + 1, :] += jnp.sum(grad * unit, axis=0, keepdims=True)
+        gacc[row + 1 : row + 2, :] += jnp.sum(grad, axis=0, keepdims=True)
+        scaled = grad * gain
+        return inverse * (
+            scaled
+            - jnp.mean(scaled, axis=-1, keepdims=True)
+            - unit * jnp.mean(scaled * unit, axis=-1, keepdims=True)
+        )
+
+    def second_norm_back(m):
+        grad = scatter_end(0, m)
+        d_mid = g_ref[m].astype(F32) + norm_back(grad, mid[m], vector(2), 2)
+        gacc[4:5, :] += jnp.sum(d_mid * attn[m], axis=0, keepdims=True)
+        attn[m] = d_mid
+        da[row_rows(m, c, y), :] = (vector(4) * d_mid).astype(BF)
+        row_start(da, 1, m)
+
+    second_norm_back(0)
+    weight_grad(1, db, hid, stage_d, own_d, zd_ref, relay_d)
+
+    def downwards(row):
+        return dot_rows(hid[pl.ds(row, 256), :], w2[...])
+
+    def attend_back(m):
+        def step(s, carry):
+            rows = block_rows(m, s)
+            before = block_rows(m, jnp.maximum(s - 1, 0))
+            d_att = dot_rows(da[rows, :], outw[...]).astype(BF)
+            here = span(s * 128, 128)
+            prior = span(jnp.maximum(s - 1, 0) * 128, 128)
+            for p in range(2):
+                d_heads = split_heads(d_att[:, 128 * p : 128 * p + 128])
+                query = split_heads(qkv[rows, pair(0, p)])
+                keys = jnp.concatenate([qkv[before, pair(1, p)], qkv[rows, pair(1, p)]], axis=0)
+                held = jnp.concatenate([qkv[before, pair(2, p)], qkv[rows, pair(2, p)]], axis=0)
+                share = probs[(m * 4 + s) * 2 + p]
+                weights = share.astype(F32)
+                d_probs = dot_rows(d_heads, held)
+                inner = jnp.sum(weights * d_probs, axis=-1, keepdims=True)
+                d_scores = (weights * (d_probs - inner) * (HD ** -0.5)).astype(BF)
+                dqs[here, pair(0, p)] = join_heads(dot(d_scores, keys))
+                d_keys = dot_cols(d_scores, query)
+                d_held = dot_cols(share, d_heads)
+                dkv[prior, pair(0, p)] += d_keys[:128]
+                dkv[prior, pair(1, p)] += d_held[:128]
+                dkv[here, pair(0, p)] = d_keys[128:]
+                dkv[here, pair(1, p)] = d_held[128:]
+            return carry
+
+        lax.fori_loop(0, 4, step, 0)
+
+        def finish(s, carry):
+            rows = block_rows(m, s)
+            here = span(s * 128, 128)
+            front, cosine, sine = expand(rows, 128)
+            for b in range(4):
+                part = dqs[here, 128 * b : 128 * b + 128] if b < 2 else dkv[here, pair(0, b - 2)]
+                qkv[rows, 128 * b : 128 * b + 128] = (
+                    part * cosine - swap(part, front) * sine
+                ).astype(BF)
+            qkv[rows, 512:768] = dkv[here, 256:512].astype(BF)
+            return carry
+
+        lax.fori_loop(0, 4, finish, 0)
+
+    def inwards(row):
+        return dot_rows(qkv[pl.ds(row, 256), :], w0[:, 0:768])
+
+    dkv[...] = jnp.zeros_like(dkv)
+    scatter(1, 0, downwards)
+    row_pass(da, 1, 0)
+    second_norm_back(1)
+    row_end(da, 1, 0)
+    attend_back(0)
+    row_scatter(1, 0, inwards)
+    scatter_pass(1, 0)
+    scatter(1, 1, downwards)
+    row_pass(da, 1, 1)
+    row_end(da, 1, 1)
+    part = dot_cols(att[...], da[...])
+    for u in range(4):
+        gsend[u] = part[:, 256 * u : 256 * u + 256].astype(BF)
+    gout[span(sq * 256, 256), :] = gsend[sq]
+    for i, k in enumerate(ROW_TEAM):
+        device, g = teams[k]
+        begin(
+            copy(gsend.at[g % 4], gout.at[span(sq * 256, 256), :], go_ss.at[i], go_rs.at[i], device)
+        )
+
+    attend_back(1)
+    row_scatter(1, 1, inwards)
+    def mine_of(values):
+        return jnp.where(xi == 0, values[:128], values[128:])
+
+    def other_of(values):
+        return jnp.where(xi == 0, values[128:], values[:128])
+
+    for i, k in enumerate(ROW_TEAM):
+        device, g = teams[k]
+        theirs = span((g % 4) * 256, 256)
+        copy(gsend.at[g % 4], gout.at[theirs, :], go_ss.at[i], go_rs.at[i], device).wait_recv()
+    for j in range(4):
+        zz = target(j)
+        begin(
+            copy(
+                gout.at[span((zz * 2 + 1 - xi) * 128, 128), :], side_o.at[j], sx_ss.at[1, j],
+                sx_rs.at[1, j], across,
+            )
+        )
+
+    def qkv_grad(j, carry):
+        part = dot_cols(n1[:, span(target(j) * 256, 256)], qkv[...])
+        send_q[j] = other_of(part).astype(BF)
+        copy(send_q.at[j], side_q.at[j], sx_ss.at[0, j], sx_rs.at[0, j], across).start()
+        keep_q[j] = mine_of(part).astype(BF)
+        return carry
+
+    lax.fori_loop(0, 4, qkv_grad, 0)
+
+
+    def summed(n, i, mine, side, stage, own, arrive, relay):
+        copy(side.at[i], side.at[i], sx_ss.at[n, i], sx_rs.at[n, i], across).wait_recv()
+        total = mine + side[i].astype(F32)
+        if i < 3:
+            stage[i] = total.astype(BF)
+            descend(2 + n, i, stage, arrive, relay)
+        else:
+            own[...] = total
+
+    def sum_q(i):
+        summed(0, i, keep_q[i].astype(F32), side_q, stage_q, own_q, zq_ref, relay_q)
+
+    def sum_o(i):
+        part = gout[span((target(i) * 2 + xi) * 128, 128), :].astype(F32)
+        summed(1, i, part, side_o, stage_o, own_o, zo_ref, relay_o)
+
+    def summed_levels(n, stage, own, arrive):
+        for i in range(3):
+            copy(stage.at[i], arrive.at[i], z_ss.at[n, i], z_rs.at[n, i], levels[0][0]).wait_send()
+        loads = [pltpu.make_async_copy(arrive.at[j], stage.at[j], loc_sem.at[j]) for j in range(3)]
+        absent = [z == 0, None, z == 3]
+        for j in range(3):
+            def load(j=j):
+                copy(
+                    stage.at[j], arrive.at[j], z_ss.at[n, j], z_rs.at[n, j], levels[0][0]
+                ).wait_recv()
+                loads[j].start()
+
+            def clear(j=j):
+                stage[j] = jnp.zeros(stage.shape[1:], BF)
+
+            if absent[j] is None:
+                load()
+            else:
+                pl.when(jnp.logical_not(absent[j]))(load)
+                pl.when(absent[j])(clear)
+        for j in range(3):
+            if absent[j] is None:
+                loads[j].wait()
+            else:
+                pl.when(jnp.logical_not(absent[j]))(loads[j].wait)
+        total = own[...].astype(F32)
+        for j in range(3):
+            total = total + stage[j].astype(F32)
+        return total.astype(BF)
+
+    def last_copies(n, pack, first, width, fin, people, who):
+        found = []
+        for i, k in enumerate(people):
+            device, g = teams[k]
+            found.append(
+                copy(
+                    pack.at[span((g % who) * 32, 32), pl.ds(first, width)],
+                    fin.at[me % who, :, pl.ds(first, width)], f_ss.at[n, i], f_rs.at[n, i], device,
+                )
+            )
+        return found
+
+    def finals(n, first, width, stage, own, arrive, pack, fin, people, who):
+        pack[:, first : first + width] = summed_levels(n, stage, own, arrive)
+        stay = pltpu.make_async_copy(
+            pack.at[span((me % who) * 32, 32), pl.ds(first, width)],
+            fin.at[me % who, :, pl.ds(first, width)], loc_sem.at[3],
+        )
+        stay.start()
+        for item in last_copies(n, pack, first, width, fin, people, who):
+            item.start()
+        stay.wait()
+
+    plans = [
+        (0, 0, 1024, stage_g, own_g, zg_ref, pack_m, fin_m, range(7), 8),
+        (1, 1024, 512, stage_d, own_d, zd_ref, pack_m, fin_m, range(7), 8),
+        (3, 768, 256, stage_o, own_o, zo_ref, pack_a, fin_a, ROW_TEAM, 4),
+        (2, 0, 768, stage_q, own_q, zq_ref, pack_a, fin_a, ROW_TEAM, 4),
+    ]
+    def first_norm_back(m):
+        grad = row_scatter_end(1, m)
+        back = norm_back(grad, x_ref[m].astype(F32), vector(0), 0)
+        dx_ref[m] = (attn[m] + back).astype(BF)
+
+    def result(m):
+        branch = scatter_end(1, m)
+        gacc[5:6, :] += jnp.sum(g_ref[m].astype(F32) * branch, axis=0, keepdims=True)
+        y_ref[m] = (mid[m] + vector(5) * branch).astype(BF)
+
+    descend_pass(0, stage_g, zg_ref, relay_g)
+    for i in range(4):
+        sum_o(i)
+    sum_q(0)
+    scatter_pass(1, 1)
+    sum_q(1)
+    descend_pass(1, stage_d, zd_ref, relay_d)
+    first_norm_back(0)
+    sum_q(2)
+    descend_pass(3, stage_o, zo_ref, relay_o)
+    first_norm_back(1)
+    sum_q(3)
+    result(0)
+    result(1)
+    for k in range(8):
+        gv_send[k] = gacc[:, 128 * k : 128 * k + 128]
+    for k, (device, g) in enumerate(teams):
+        begin(copy(gv_send.at[g], gv_in.at[k], gv_ss.at[k], gv_rs.at[k], device))
+
+    descend_pass(2, stage_q, zq_ref, relay_q)
+    for item in pack_sends:
+        item.wait_send()
+    finals(*plans[0])
+    for item in pending:
+        if isinstance(item, tuple):
+            pl.when(jnp.logical_not(item[0]))(item[1].wait_send)
+        else:
+            item.wait_send()
+    for j in range(4):
+        copy(send_q.at[j], side_q.at[j], sx_ss.at[0, j], sx_rs.at[0, j], across).wait_send()
+    for k, (device, g) in enumerate(teams):
+        copy(gv_send.at[g], gv_in.at[k], gv_ss.at[k], gv_rs.at[k], device).wait_recv()
+    total = gv_send[me]
+    for k in range(7):
+        total = total + gv_in[k]
+    gv_z[0] = total
+    level_sends = []
+    for j, (device, _) in enumerate(levels):
+        item = copy(gv_z.at[0], gv_z.at[1 + j], gv_ss.at[7 + j], gv_rs.at[7 + j], device)
+        item.start()
+        level_sends.append(item)
+    finals(*plans[1])
+    for item in level_sends:
+        item.wait()
+    gv_all[me] = gv_z[0] + gv_z[1] + gv_z[2] + gv_z[3]
+    for k, (device, g) in enumerate(teams):
+        copy(gv_all.at[me], gv_all.at[me], gv_ss.at[10 + k], gv_rs.at[10 + k], device).start()
+    finals(*plans[2])
+    finals(*plans[3])
+    for k, (device, g) in enumerate(teams):
+        copy(gv_all.at[g], gv_all.at[g], gv_ss.at[10 + k], gv_rs.at[10 + k], device).wait()
+    vg_ref[...] = gv_all[z * 2 + me // 4]
+    for n, first, width, _, _, _, pack, fin, people, who in plans:
+        for item in last_copies(n, pack, first, width, fin, people, who):
+            item.wait()
+
+
+def layer_fast(
+    block_input,
+    positions,
+    out_grad,
+    qkv_weight,
+    out_weight,
+    gate_weight,
+    up_weight,
+    down_weight,
+    norm1_gain,
+    norm1_shift,
+    norm2_gain,
+    norm2_shift,
+    attn_scale,
+    mlp_scale,
+):
+    vectors = jnp.stack(
+        [norm1_gain, norm1_shift, norm2_gain, norm2_shift, attn_scale, mlp_scale]
+    ).astype(F32)
+    packed = jnp.concatenate([jnp.tile(vectors, (1, 4)), positions.astype(F32)], axis=0)
+    vmem, anywhere = pl.BlockSpec(memory_space=pltpu.VMEM), pl.BlockSpec(memory_space=pl.ANY)
+    dma = pltpu.SemaphoreType.DMA
+    scratch = [
+        pltpu.VMEM((4, 8, 8, 128), F32), pltpu.VMEM((8, 1024), F32), pltpu.VMEM((8, 1024), F32),
+        pltpu.VMEM((7, 8, 128), F32), pltpu.VMEM((4, 8, 128), F32), pltpu.VMEM((8, 8, 128), F32),
+        pltpu.VMEM((8, 8, 128), F32),
+        pltpu.VMEM((128, 1024), BF), pltpu.VMEM((256, 1536), BF), pltpu.VMEM((1024, 1024), BF),
+        pltpu.VMEM((1024, 1024), BF), pltpu.VMEM((1024, 512), BF), pltpu.VMEM((256, 1024), BF),
+        pltpu.VMEM((1024, 1024), BF), pltpu.VMEM((2048, 1024), BF), pltpu.VMEM((2048, 1024), BF),
+        pltpu.VMEM((1024, 1024), BF),
+        pltpu.VMEM((1024, 768), BF), pltpu.VMEM((1024, 256), BF), pltpu.VMEM((16, 256, 256), BF),
+        pltpu.VMEM((512, 256), F32), pltpu.VMEM((512, 512), F32),
+        pltpu.VMEM((2048, 512), BF), pltpu.VMEM((2048, 1024), BF),
+        pltpu.VMEM((2, 512, 1024), BF), pltpu.VMEM((2, 2, 512, 1024), BF),
+        pltpu.VMEM((2, 2, 3, 128, 1024), BF), pltpu.VMEM((2, 256, 1024), BF),
+        pltpu.VMEM((2, 256, 1024), BF), pltpu.VMEM((2, 256, 1024), BF),
+        pltpu.VMEM((2, 128, 1024), BF),
+        pltpu.VMEM((3, 128, 768), BF), pltpu.VMEM((3, 128, 256), BF),
+        pltpu.VMEM((3, 256, 1024), BF), pltpu.VMEM((3, 256, 512), BF),
+        pltpu.VMEM((128, 768), F32), pltpu.VMEM((128, 256), F32),
+        pltpu.VMEM((256, 1024), BF), pltpu.VMEM((256, 512), BF),
+        pltpu.VMEM((1024, 256), BF), pltpu.VMEM((4, 256, 256), BF),
+        pltpu.VMEM((4, 128, 768), BF), pltpu.VMEM((4, 128, 256), BF),
+        pltpu.VMEM((4, 128, 768), BF), pltpu.VMEM((4, 128, 768), BF),
+        pltpu.VMEM((256, 1024), BF), pltpu.VMEM((256, 512), BF), pltpu.VMEM((128, 768), BF),
+        pltpu.VMEM((128, 256), BF),
+        pltpu.VMEM((2, 128, 1024), F32), pltpu.VMEM((2, 128, 1024), F32),
+        pltpu.VMEM((1024, 128), F32), pltpu.VMEM((1024, 128), F32),
+        dma((10,)), dma((10,)), dma((3,)), dma((3,)), dma((2, 8)), dma((2, 8)), dma((2, 11)), dma((2, 11)),
+        dma((3,)), dma((3,)), dma((2, 2, 3)), dma((2, 2, 3)), dma((2, 2, 7)), dma((2, 2, 7)),
+        dma((2, 2, 2)), dma((2, 2, 2)), dma((2, 2, 5)), dma((2, 2, 5)), dma((3,)), dma((3,)),
+        dma((2, 4)), dma((2, 4)), dma((4, 4)), dma((4, 4)), dma((4, 7)), dma((4, 7)),
+        dma((17,)), dma((17,)), dma((4,)),
+    ]
+    y, dx, vg, fin_a, fin_m = pl.pallas_call(
+        layer_kernel,
+        out_shape=(
+            jax.ShapeDtypeStruct((2, 128, 1024), BF),
+            jax.ShapeDtypeStruct((2, 128, 1024), BF),
+            jax.ShapeDtypeStruct((8, 128), F32),
+            jax.ShapeDtypeStruct((4, 32, 1024), BF),
+            jax.ShapeDtypeStruct((8, 32, 1536), BF),
+            jax.ShapeDtypeStruct((3, 128, 768), BF),
+            jax.ShapeDtypeStruct((3, 128, 256), BF),
+            jax.ShapeDtypeStruct((3, 256, 1024), BF),
+            jax.ShapeDtypeStruct((3, 256, 512), BF),
+        ),
+        in_specs=[vmem] * 9,
+        out_specs=(vmem, vmem, vmem) + (anywhere,) * 6,
+        scratch_shapes=scratch,
+        compiler_params=pltpu.CompilerParams(
+            collective_id=0, has_side_effects=True, vmem_limit_bytes=VMEM_BYTES
+        ),
+        cost_estimate=pl.CostEstimate(
+            flops=26_000_000_000, bytes_accessed=8_000_000, transcendentals=4_000_000
+        ),
+        name="layer",
+    )(
+        block_input, out_grad, packed, jnp.asarray(trig_table()), qkv_weight, out_weight,
+        gate_weight, up_weight, down_weight.T,
+    )[:5]
+    fin_a, fin_m = fin_a.astype(F32), fin_m.astype(F32)
+    grad_qkv = (
+        fin_a[:, :, 0:768].reshape(4, 32, 3, 256).transpose(1, 2, 0, 3).reshape(32, 3072)
+    )
+    grad_out = fin_a[:, :, 768:1024].transpose(1, 0, 2).reshape(32, 1024)
+    grad_gate = fin_m[:, :, 0:512].transpose(1, 0, 2).reshape(32, 4096)
+    grad_up = fin_m[:, :, 512:1024].transpose(1, 0, 2).reshape(32, 4096)
+    grad_down = fin_m[:, :, 1024:1536].transpose(0, 2, 1).reshape(4096, 32)
+    part = lax.axis_index(("dp", "seq")) % 4
+    vg = lax.dynamic_index_in_dim(vg.reshape(8, 4, 32), part, 1, keepdims=False)
+    return (y, dx, grad_qkv, grad_out, grad_gate, grad_up, grad_down) + tuple(
+        vg[i] for i in range(6)
+    )
+
+
+def fits(mesh):
+    return mesh.shape["dp"] == 8 and mesh.shape["seq"] == 4
+
+
 def solution(mesh):
     return jax.shard_map(
-        body,
+        layer_fast if fits(mesh) else body,
         mesh=mesh,
         in_specs=(
             P(None, ("dp", "seq"), None),

time: 2120 us -> 234 us (0.11)
  waiting for transfers between devices: 1410 us -> 0 us
  local copies, waits for them, and re-layouts: 386 us -> 8.86 us
  Pallas kernels: 0 us -> 223 us
  matrix products: 221 us -> 0 us
  starting transfers between devices: 31.8 us -> 0 us
  other arithmetic: 28.9 us -> 1.5 us
    unnamed x5 -> x0, waiting for transfers between devices: 1050 us -> none
    all_gather x1 -> x0, waiting for transfers between devices: 345 us -> none  [body(): lax.all_gather(packed, ('dp', 'seq'), axis=0, tiled=True)]
    pallas_call x0 -> x1, Pallas kernels: none -> 223 us  [layer_fast(): pl.pallas_call(layer_kernel, out_shape=(jax.ShapeDtypeStruct((2, 128, 102...]
    dot_general x42 -> x0, matrix products: 221 us -> none  [the longest x2 36 us: step(): jnp.einsum('hqk,khd->qhd', grad_scores, block_keys, preferred_element_typ...]
    unnamed x224 -> x14, local copies, waits for them, and re-layouts: 110 us -> 1.79 us
    reshape x16 -> x7, local copies, waits for them, and re-layouts: 107 us -> 4.41 us  [the longest x2 1.16 us: layer_fast(): fin_a[:, :, 0:768].reshape(4, 32, 3, 256).transpose(1, 2, 0, 3)]
    concatenate x7 -> x0, local copies, waits for them, and re-layouts: 76.2 us -> none  [the longest x6 74.8 us: pack_grads(): return jnp.concatenate(pieces, axis=1)]
    slice x29 -> x1, local copies, waits for them, and re-layouts: 47.8 us -> 1.02 us  [layer_fast(): fin_a[:, :, 0:768].reshape(4, 32, 3, 256).transpose(1, 2, 0, 3)]
  transfers between devices with their start and end apart: 11 -> 0, of which waited for: 5 -> 0; matrix products, arithmetic and copies ran while one was open for 17% -> 0% of each run, Pallas kernels for 0% -> 0%
where the time goes in v1:
time: 234 us
  Pallas kernels  223 us (95%)
  local copies, waits for them, and re-layouts  8.86 us (4%)
    pallas_call x1, Pallas kernels, layer_fast(): pl.pallas_call(layer_kernel, out_shape=(jax.ShapeDtypeStruct((2, 128, 102...  223 us

profile of v1, /device:TPU:0, one launch (start us, length us, event | category | flops | bytes accessed | tf_op | source)
XLA Modules:
  0.0 234.1 jit_solution(4139147283560199816)
XLA Ops:
  0.6 0.7 convert_element_type.17
  1.3 0.8 stack.27
  2.1 0.1 tile.10
  2.2 0.6 pad_maximum_fusion.vec_ref
  2.8 223.0 %layer.1 = (bf16[2,128,1024]{2,1,0:T(8,128)(2,1)}, bf16[2,128,1024]{2,1,0:T(8,128)(2,1)}, f32[8,128]{1,0:T(8,128)}, bf16[4,32,1024]{2,1,0:T(8,128)(2,1)}, bf16[8...) custom-call(bf16[2,128,1024]{2,1,0:T(8,128)(2,1)} %x_ref.1, ...), custom_call_target="tpu_custom_call" | custom-call | flops 25999998976 | bytes 8000000 | tf_op jit(solution)/shard_map/layer/pallas_call | solution.py:1387
  225.8 0.0 copy-start
  225.8 1.0 slice.50
  226.8 0.2 reshape.111
  227.0 0.0 copy-start.1
  227.1 0.3 copy.33
  227.3 0.9 reshape.112
  228.3 0.0 copy-done
  228.3 0.7 copy.38
  229.0 0.0 copy-done.1
  229.0 0.2 convert_element_type.19
  229.2 0.2 slice_bitcast_fusion
  229.4 0.0 copy-start.4
  229.4 0.0 copy-start.3
  229.4 0.8 copy.39
  230.2 0.0 copy-start.2
  230.2 0.8 copy.40
  231.1 0.8 copy.41
  231.9 0.0 copy-done.4
  231.9 0.1 reshape.117
  232.0 0.5 fusion
  232.5 0.0 copy-done.3
  232.5 0.8 copy.44
  233.3 0.0 copy-done.2
  233.3 0.8 copy.45
  (3 shorter events, 0.1 us)
Async XLA Ops:
  225.8 2.5 %copy-start = (bf16[4,32,1024]{2,1,0:T(8,128)(2,1)S(1)}, bf16[4,32,1024]{2,1,0:T(8,128)(2,1)}, u32[]{:S(2)}) copy-start(bf16[4,32,1024]{2,1,0:T(8,128)(2,1)} %get-tuple-element.20) | copy-start | bytes 786436
  227.0 2.0 copy-start.1
  229.4 2.5 %copy-start.4 = (f32[8,128]{1,0:T(8,128)S(1)}, f32[8,128]{1,0:T(8,128)}, u32[]{:S(2)}) copy-start(f32[8,128]{1,0:T(8,128)} %get-tuple-element.22) | copy-start | bytes 12292
  229.4 3.1 %copy-start.3 = (bf16[2,128,1024]{2,1,0:T(8,128)(2,1)S(1)}, bf16[2,128,1024]{2,1,0:T(8,128)(2,1)}, u32[]{:S(2)}) copy-start(bf16[2,128,1024]{2,1,0:T(8,128)(2,1)} %get-tuple-element.45) | copy-start | bytes 1572868
  230.2 3.1 %copy-start.2 = (bf16[2,128,1024]{2,1,0:T(8,128)(2,1)S(1)}, bf16[2,128,1024]{2,1,0:T(8,128)(2,1)}, u32[]{:S(2)}) copy-start(bf16[2,128,1024]{2,1,0:T(8,128)(2,1)} %get-tuple-element.46) | copy-start | bytes 1572868

commit v2 on v1

--- a/solution.py
+++ b/solution.py
@@ -670,6 +670,7 @@
         rows = w0.at[span((z * 8 + g) * 32, 32), :]
         copy(rows, rows, wr_ss.at[i], wr_rs.at[i], device).wait_recv()
     slab_up(0)
+    weights_out(0)
     for j in range(3):
         block = vec_all.at[sources[j]]
         copy(block, block, vec_ss.at[7 + j], vec_rs.at[7 + j], levels[j][0]).wait_recv()
@@ -753,7 +754,6 @@
         return carry
 
     lax.fori_loop(0, 8, make_trig, 0)
-    weights_out(0)
 
     def expand(rows, count):
         both = trig[rows, :]
@@ -767,11 +767,11 @@
 
     slab_pass(0)
     slab_up(1)
+    weights_up(0)
     row_pass(n1, 0, 0)
     row_pass(n1, 0, 1)
     gather_pass(db, 0, 0, 1)
     weights_out(1)
-    weights_up(0)
     slab_in(0)
 
     first_head = lax.broadcasted_iota(jnp.int32, (128, 128), 1) < 64
@@ -956,7 +956,6 @@
             )
         )
     outw[:, span(sq * 256, 256)] = w0[span(sq * 256, 256), 768:1024]
-    gather_start(db, 0, 1)
     row_end(n1, 0, 1)
     project(1)
     for i, k in enumerate(ROW_TEAM):
@@ -966,6 +965,7 @@
             outw.at[:, span((g % 4) * 256, 256)], o_ss.at[i], o_rs.at[i], device,
         ).wait_recv()
     row_scatter(0, 0, outwards)
+    gather_start(db, 0, 1)
     weights_up(1)
     attend(1)
     row_scatter(0, 1, outwards)

time: 234 us -> 221 us (0.944)
  Pallas kernels: 223 us -> 209 us
    pallas_call x1, Pallas kernels: 223 us -> 209 us  [layer_fast(): pl.pallas_call(layer_kernel, out_shape=(jax.ShapeDtypeStruct((2, 128, 102...]
where the time goes in v2:
time: 221 us; the launch traced here: 220 us
  Pallas kernels  209 us (95%)
  local copies, waits for them, and re-layouts  8.86 us (4%)
    pallas_call x1, Pallas kernels, layer_fast(): pl.pallas_call(layer_kernel, out_shape=(jax.ShapeDtypeStruct((2, 128, 102...  209 us

profile of v2, /device:TPU:0, one launch (start us, length us, event | category | flops | bytes accessed | tf_op | source)
XLA Modules:
  0.0 220.4 jit_solution(11668226703605268990)
XLA Ops:
  0.6 0.7 convert_element_type.17
  1.3 0.8 stack.27
  2.1 0.1 tile.10
  2.2 0.6 pad_maximum_fusion.vec_ref
  2.8 209.3 %layer.1 = (bf16[2,128,1024]{2,1,0:T(8,128)(2,1)}, bf16[2,128,1024]{2,1,0:T(8,128)(2,1)}, f32[8,128]{1,0:T(8,128)}, bf16[4,32,1024]{2,1,0:T(8,128)(2,1)}, bf16[8...) custom-call(bf16[2,128,1024]{2,1,0:T(8,128)(2,1)} %x_ref.1, ...), custom_call_target="tpu_custom_call" | custom-call | flops 25999998976 | bytes 8000000 | tf_op jit(solution)/shard_map/layer/pallas_call | solution.py:1387
  212.1 0.0 copy-start
  212.1 1.0 slice.50
  213.1 0.2 reshape.111
  213.3 0.0 copy-start.1
  213.3 0.3 copy.33
  213.6 0.9 reshape.112
  214.5 0.0 copy-done
  214.6 0.7 copy.38
  215.3 0.0 copy-done.1
  215.3 0.2 convert_element_type.19
  215.5 0.2 slice_bitcast_fusion
  215.6 0.0 copy-start.4
  215.6 0.0 copy-start.3
  215.7 0.8 copy.39
  216.5 0.0 copy-start.2
  216.5 0.8 copy.40
  217.3 0.8 copy.41
  218.2 0.0 copy-done.4
  218.2 0.1 reshape.117
  218.2 0.5 fusion
  218.8 0.0 copy-done.3
  218.8 0.8 copy.44
  219.6 0.0 copy-done.2
  219.6 0.8 copy.45
  (3 shorter events, 0.1 us)
Async XLA Ops:
  212.1 2.5 %copy-start = (bf16[4,32,1024]{2,1,0:T(8,128)(2,1)S(1)}, bf16[4,32,1024]{2,1,0:T(8,128)(2,1)}, u32[]{:S(2)}) copy-start(bf16[4,32,1024]{2,1,0:T(8,128)(2,1)} %get-tuple-element.20) | copy-start | bytes 786436
  213.3 2.0 copy-start.1
  215.6 2.5 %copy-start.4 = (f32[8,128]{1,0:T(8,128)S(1)}, f32[8,128]{1,0:T(8,128)}, u32[]{:S(2)}) copy-start(f32[8,128]{1,0:T(8,128)} %get-tuple-element.22) | copy-start | bytes 12292
  215.6 3.1 %copy-start.3 = (bf16[2,128,1024]{2,1,0:T(8,128)(2,1)S(1)}, bf16[2,128,1024]{2,1,0:T(8,128)(2,1)}, u32[]{:S(2)}) copy-start(bf16[2,128,1024]{2,1,0:T(8,128)(2,1)} %get-tuple-element.45) | copy-start | bytes 1572868
  216.5 3.1 %copy-start.2 = (bf16[2,128,1024]{2,1,0:T(8,128)(2,1)S(1)}, bf16[2,128,1024]{2,1,0:T(8,128)(2,1)}, u32[]{:S(2)}) copy-start(bf16[2,128,1024]{2,1,0:T(8,128)(2,1)} %get-tuple-element.46) | copy-start | bytes 1572868

commit v3 on v2

--- a/solution.py
+++ b/solution.py
@@ -1144,6 +1144,7 @@
     attend_back(0)
     row_scatter(1, 0, inwards)
     scatter_pass(1, 0)
+    descend_pass(0, stage_g, zg_ref, relay_g)
     scatter(1, 1, downwards)
     row_pass(da, 1, 1)
     row_end(da, 1, 1)
@@ -1273,13 +1274,12 @@
         gacc[5:6, :] += jnp.sum(g_ref[m].astype(F32) * branch, axis=0, keepdims=True)
         y_ref[m] = (mid[m] + vector(5) * branch).astype(BF)
 
-    descend_pass(0, stage_g, zg_ref, relay_g)
     for i in range(4):
         sum_o(i)
+    descend_pass(1, stage_d, zd_ref, relay_d)
     sum_q(0)
     scatter_pass(1, 1)
     sum_q(1)
-    descend_pass(1, stage_d, zd_ref, relay_d)
     first_norm_back(0)
     sum_q(2)
     descend_pass(3, stage_o, zo_ref, relay_o)

time: 221 us -> 219 us (level)
  no operation moved by 1% of the time
where the time goes in v3:
time: 219 us
  Pallas kernels  208 us (95%)
  local copies, waits for them, and re-layouts  8.86 us (4%)
    pallas_call x1, Pallas kernels, layer_fast(): pl.pallas_call(layer_kernel, out_shape=(jax.ShapeDtypeStruct((2, 128, 102...  208 us

profile of v3, /device:TPU:0, one launch (start us, length us, event | category | flops | bytes accessed | tf_op | source)
XLA Modules:
  0.0 219.1 jit_solution(14857013428629476097)
XLA Ops:
  0.6 0.7 convert_element_type.17
  1.3 0.8 stack.27
  2.1 0.1 tile.10
  2.2 0.6 pad_maximum_fusion.vec_ref
  2.8 208.0 %layer.1 = (bf16[2,128,1024]{2,1,0:T(8,128)(2,1)}, bf16[2,128,1024]{2,1,0:T(8,128)(2,1)}, f32[8,128]{1,0:T(8,128)}, bf16[4,32,1024]{2,1,0:T(8,128)(2,1)}, bf16[8...) custom-call(bf16[2,128,1024]{2,1,0:T(8,128)(2,1)} %x_ref.1, ...), custom_call_target="tpu_custom_call" | custom-call | flops 25999998976 | bytes 8000000 | tf_op jit(solution)/shard_map/layer/pallas_call | solution.py:1387
  210.8 0.0 copy-start
  210.8 1.0 slice.50
  211.8 0.2 reshape.111
  212.0 0.0 copy-start.1
  212.0 0.3 copy.33
  212.3 0.9 reshape.112
  213.2 0.0 copy-done
  213.3 0.7 copy.38
  214.0 0.0 copy-done.1
  214.0 0.2 convert_element_type.19
  214.2 0.2 slice_bitcast_fusion
  214.3 0.0 copy-start.4
  214.3 0.0 copy-start.3
  214.3 0.8 copy.39
  215.2 0.0 copy-start.2
  215.2 0.8 copy.40
  216.0 0.8 copy.41
  216.9 0.0 copy-done.4
  216.9 0.1 reshape.117
  216.9 0.5 fusion
  217.5 0.0 copy-done.3
  217.5 0.8 copy.44
  218.3 0.0 copy-done.2
  218.3 0.8 copy.45
  (3 shorter events, 0.1 us)
Async XLA Ops:
  210.8 2.5 %copy-start = (bf16[4,32,1024]{2,1,0:T(8,128)(2,1)S(1)}, bf16[4,32,1024]{2,1,0:T(8,128)(2,1)}, u32[]{:S(2)}) copy-start(bf16[4,32,1024]{2,1,0:T(8,128)(2,1)} %get-tuple-element.20) | copy-start | bytes 786436
  212.0 2.0 copy-start.1
  214.3 2.5 %copy-start.4 = (f32[8,128]{1,0:T(8,128)S(1)}, f32[8,128]{1,0:T(8,128)}, u32[]{:S(2)}) copy-start(f32[8,128]{1,0:T(8,128)} %get-tuple-element.22) | copy-start | bytes 12292
  214.3 3.1 %copy-start.3 = (bf16[2,128,1024]{2,1,0:T(8,128)(2,1)S(1)}, bf16[2,128,1024]{2,1,0:T(8,128)(2,1)}, u32[]{:S(2)}) copy-start(bf16[2,128,1024]{2,1,0:T(8,128)(2,1)} %get-tuple-element.45) | copy-start | bytes 1572868
  215.2 3.1 %copy-start.2 = (bf16[2,128,1024]{2,1,0:T(8,128)(2,1)S(1)}, bf16[2,128,1024]{2,1,0:T(8,128)(2,1)}, u32[]{:S(2)}) copy-start(bf16[2,128,1024]{2,1,0:T(8,128)(2,1)} %get-tuple-element.46) | copy-start | bytes 1572868

commit v4 on v3

--- a/solution.py
+++ b/solution.py
@@ -1282,6 +1282,7 @@
     sum_q(1)
     first_norm_back(0)
     sum_q(2)
+    descend_pass(2, stage_q, zq_ref, relay_q)
     descend_pass(3, stage_o, zo_ref, relay_o)
     first_norm_back(1)
     sum_q(3)
@@ -1292,7 +1293,6 @@
     for k, (device, g) in enumerate(teams):
         begin(copy(gv_send.at[g], gv_in.at[k], gv_ss.at[k], gv_rs.at[k], device))
 
-    descend_pass(2, stage_q, zq_ref, relay_q)
     for item in pack_sends:
         item.wait_send()
     finals(*plans[0])

time: 219 us -> 219 us (level)
  no operation moved by 1% of the time
where the time goes in v4:
time: 219 us
  Pallas kernels  208 us (95%)
  local copies, waits for them, and re-layouts  8.86 us (4%)
    pallas_call x1, Pallas kernels, layer_fast(): pl.pallas_call(layer_kernel, out_shape=(jax.ShapeDtypeStruct((2, 128, 102...  208 us

profile of v4, /device:TPU:0, one launch (start us, length us, event | category | flops | bytes accessed | tf_op | source)
XLA Modules:
  0.0 219.1 jit_solution(5544578324683401910)
XLA Ops:
  0.6 0.7 convert_element_type.17
  1.3 0.8 stack.27
  2.1 0.1 tile.10
  2.2 0.6 pad_maximum_fusion.vec_ref
  2.8 208.0 %layer.1 = (bf16[2,128,1024]{2,1,0:T(8,128)(2,1)}, bf16[2,128,1024]{2,1,0:T(8,128)(2,1)}, f32[8,128]{1,0:T(8,128)}, bf16[4,32,1024]{2,1,0:T(8,128)(2,1)}, bf16[8...) custom-call(bf16[2,128,1024]{2,1,0:T(8,128)(2,1)} %x_ref.1, ...), custom_call_target="tpu_custom_call" | custom-call | flops 25999998976 | bytes 8000000 | tf_op jit(solution)/shard_map/layer/pallas_call | solution.py:1387
  210.8 0.0 copy-start
  210.8 1.0 slice.50
  211.8 0.2 reshape.111
  212.0 0.0 copy-start.1
  212.0 0.3 copy.33
  212.3 0.9 reshape.112
  213.2 0.0 copy-done
  213.3 0.7 copy.38
  214.0 0.0 copy-done.1
  214.0 0.2 convert_element_type.19
  214.2 0.2 slice_bitcast_fusion
  214.3 0.0 copy-start.4
  214.3 0.0 copy-start.3
  214.3 0.8 copy.39
  215.2 0.0 copy-start.2
  215.2 0.8 copy.40
  216.0 0.8 copy.41
  216.9 0.0 copy-done.4
  216.9 0.1 reshape.117
  216.9 0.5 fusion
  217.5 0.0 copy-done.3
  217.5 0.8 copy.44
  218.3 0.0 copy-done.2
  218.3 0.8 copy.45
  (3 shorter events, 0.1 us)
Async XLA Ops:
  210.8 2.5 %copy-start = (bf16[4,32,1024]{2,1,0:T(8,128)(2,1)S(1)}, bf16[4,32,1024]{2,1,0:T(8,128)(2,1)}, u32[]{:S(2)}) copy-start(bf16[4,32,1024]{2,1,0:T(8,128)(2,1)} %get-tuple-element.20) | copy-start | bytes 786436
  212.0 2.0 copy-start.1
  214.3 2.5 %copy-start.4 = (f32[8,128]{1,0:T(8,128)S(1)}, f32[8,128]{1,0:T(8,128)}, u32[]{:S(2)}) copy-start(f32[8,128]{1,0:T(8,128)} %get-tuple-element.22) | copy-start | bytes 12292
  214.3 3.1 %copy-start.3 = (bf16[2,128,1024]{2,1,0:T(8,128)(2,1)S(1)}, bf16[2,128,1024]{2,1,0:T(8,128)(2,1)}, u32[]{:S(2)}) copy-start(bf16[2,128,1024]{2,1,0:T(8,128)(2,1)} %get-tuple-element.45) | copy-start | bytes 1572868
  215.2 3.1 %copy-start.2 = (bf16[2,128,1024]{2,1,0:T(8,128)(2,1)S(1)}, bf16[2,128,1024]{2,1,0:T(8,128)(2,1)}, u32[]{:S(2)}) copy-start(bf16[2,128,1024]{2,1,0:T(8,128)(2,1)} %get-tuple-element.46) | copy-start | bytes 1572868
